TPU v7x, 256 devices: a whole 4x4x8 slice. The times are simulated.
256 devices in a mesh: ctx: 32 (over x, y, core), tp: 8 (over z).
Axes of the slice: x: 4, y: 4, z: 8, core: 2. Of those that a mesh axis runs over, the one named last changes fastest.
Arguments:
- query_proj: bfloat16 [4096, 8192], P('ctx', 'tp'), may hold values from -6 to 6
- key_proj: bfloat16 [4096, 8192], P('ctx', 'tp'), may hold values from -6 to 6
- value_proj: bfloat16 [4096, 8192], P('ctx', 'tp'), may hold values from -6 to 6
- grad_out: bfloat16 [4096, 8192], P('ctx', 'tp'), may hold values from -6 to 6
- residues: float32 [512, 16], P(('ctx', 'tp')), may hold values from -1 to 1
- decay_time: float32 [512, 16], P(('ctx', 'tp')), may hold values from 30 to 20480
- doc_lengths: int32 [4], replicated, may hold values from 1 to 2048, 4096 in all
Outputs:
- mixed: bfloat16 [4096, 8192], P('ctx', 'tp')
- grad_query: bfloat16 [4096, 8192], P('ctx', 'tp')
- grad_key: bfloat16 [4096, 8192], P('ctx', 'tp')
- grad_value: bfloat16 [4096, 8192], P('ctx', 'tp')
- grad_residues: float32 [512, 16], P(('ctx', 'tp'))
Inputs may be any that keep to these rules, and one draw needn't show every extreme that they name: `doc_lengths`: each document holds at least one token; the longest holds exactly half of 4096.
All inputs are finite; a program needn't handle non-finite values.
Results may differ from a plain program's by a relative error of at most 0.0015.
Values sent between devices are 32-bit elements; how exact they have to be, the bound alone decides.
A program may use at most 128 MiB of HBM per device.

v0:
```python
import jax
import jax.numpy as jnp
from jax import lax
from jax.sharding import PartitionSpec as P

GROUP = 16
MODES = 16
BLOCK = 128


HIGHEST = lax.Precision.HIGHEST


def entering(value, axis, join, neutral, backward):
    count, mine = (lax.axis_size(axis), lax.axis_index(axis))
    pieces = jax.tree.map(lambda part: lax.all_gather(part, axis), value)
    if backward:
        pieces = jax.tree.map(lambda part: part[::-1], pieces)
        mine = count - 1 - mine
    so_far = jax.tree.map(
        lambda part, zero: jnp.full_like(part, 0) + jnp.asarray(zero, part.dtype), value, neutral
    )

    def lap(position, so_far):
        longer = join(so_far, jax.tree.map(lambda part: part[position], pieces))
        return jax.tree.map(lambda new, old: jnp.where(position < mine, new, old), longer, so_far)

    return lax.fori_loop(0, count - 1, lap, so_far)


def doc_index(positions, doc_ends):
    return jnp.sum((positions[..., None] >= doc_ends).astype(jnp.int32), axis=-1)


def chain(earlier, later_part):
    return (earlier[0] * later_part[0], later_part[0][..., None] * earlier[1] + later_part[1])


def per_device(query_proj, key_proj, value_proj, grad_out, residues, decay_time, doc_lengths):
    tokens, channels = query_proj.shape
    groups_dev = channels // GROUP
    blocks = tokens // BLOCK
    ctx_count = lax.axis_size("ctx")
    tp_count = lax.axis_size("tp")
    ctx_pos = lax.axis_index("ctx")
    tp_pos = lax.axis_index("tp")
    seq_len = tokens * ctx_count
    all_res, all_time = (
        lax.all_gather(residues, ("ctx", "tp"), axis=0, tiled=True),
        lax.all_gather(decay_time, ("ctx", "tp"), axis=0, tiled=True),
    )
    res_dev = lax.dynamic_slice_in_dim(all_res, tp_pos * groups_dev, groups_dev, 0)
    rate_dev = 1.0 / lax.dynamic_slice_in_dim(all_time, tp_pos * groups_dev, groups_dev, 0)
    doc_ends = jnp.cumsum(doc_lengths)
    first_pos = ctx_pos * tokens
    local_pos = jnp.arange(tokens, dtype=jnp.int32)
    doc_ids = doc_index(first_pos + local_pos, doc_ends)
    docs_blk = doc_ids.reshape(blocks, BLOCK)
    blk_first = first_pos + jnp.arange(blocks, dtype=jnp.int32) * BLOCK
    blk_before = doc_index(blk_first - 1, doc_ends)
    blk_after = doc_index(blk_first + BLOCK, doc_ends)
    shard_before = doc_index(first_pos - 1, doc_ends)
    shard_after = doc_index(first_pos + tokens, doc_ends)
    shape4 = (blocks, BLOCK, groups_dev, GROUP)
    query_wide = query_proj.astype(jnp.float32).reshape(shape4)
    key_wide = key_proj.astype(jnp.float32).reshape(shape4)
    value_wide = value_proj.astype(jnp.float32).reshape(shape4)
    grad_wide = grad_out.astype(jnp.float32).reshape(shape4)
    mixture = key_wide * value_wide
    dconv = grad_wide * query_wide
    lag_index = jnp.arange(BLOCK, dtype=jnp.int32)
    lag_float = lag_index.astype(jnp.float32)
    offset = lag_index[:, None] - lag_index[None, :]
    onehot = (offset[None] == lag_index[:, None, None]).astype(jnp.float32)
    powers = jnp.exp(-rate_dev[:, :, None] * lag_float)
    filter_taps = jnp.einsum("gm,gmk->gk", res_dev, powers, precision=HIGHEST)
    toeplitz = jnp.einsum("gk,kts->gts", filter_taps, onehot, precision=HIGHEST)
    same_doc = ((docs_blk[:, :, None] == docs_blk[:, None, :]) & (offset >= 0)[None]).astype(
        jnp.float32
    )
    kernel = toeplitz[None] * same_doc[:, None]
    block_decay = jnp.exp(-rate_dev * BLOCK)
    zero_state = jnp.zeros((groups_dev, MODES, GROUP), jnp.float32)
    unit_decay = jnp.ones((groups_dev, MODES), jnp.float32)

    def fold_blocks(state_acc, block_item):
        return (block_item[0][..., None] * state_acc + block_item[1], state_acc)

    convolved = jnp.einsum("bgts,bsgc->btgc", kernel, mixture, precision=HIGHEST)
    end_mask = (docs_blk == docs_blk[:, -1:]).astype(jnp.float32)
    end_weight = (
        jnp.exp(-rate_dev[None, None] * (BLOCK - 1.0 - lag_float)[None, :, None, None])
        * end_mask[:, :, None, None]
    )
    blk_states = jnp.einsum("bsgm,bsgc->bgmc", end_weight, mixture, precision=HIGHEST)
    blk_decay = (
        block_decay[None] * (docs_blk[:, -1] == blk_before).astype(jnp.float32)[:, None, None]
    )
    shard_state, _ = lax.scan(fold_blocks, zero_state, (blk_decay, blk_states))
    shard_decay = jnp.exp(-rate_dev * tokens) * (doc_ids[-1] == shard_before).astype(jnp.float32)
    dmix = jnp.einsum("bgts,btgc->bsgc", kernel, dconv, precision=HIGHEST)
    start_mask = (docs_blk == docs_blk[:, :1]).astype(jnp.float32)
    start_weight = (
        jnp.exp(-rate_dev[None, None] * lag_float[None, :, None, None])
        * start_mask[:, :, None, None]
    )
    blk_back = jnp.einsum("btgm,btgc->bgmc", start_weight, dconv, precision=HIGHEST)
    blk_back_decay = (
        block_decay[None] * (docs_blk[:, 0] == blk_after).astype(jnp.float32)[:, None, None]
    )
    shard_back, _ = lax.scan(fold_blocks, zero_state, (blk_back_decay, blk_back), reverse=True)
    shard_back_decay = jnp.exp(-rate_dev * tokens) * (doc_ids[0] == shard_after).astype(jnp.float32)
    carry_in = entering((shard_decay, shard_state), "ctx", chain, (unit_decay, zero_state), False)[
        1
    ]
    carry_out = entering(
        (shard_back_decay, shard_back), "ctx", chain, (unit_decay, zero_state), True
    )[1]
    _, blk_in = lax.scan(fold_blocks, carry_in, (blk_decay, blk_states))
    prev_mask = (docs_blk == blk_before[:, None]).astype(jnp.float32)
    lead_weight = (
        jnp.exp(-rate_dev[None, None] * (lag_float + 1.0)[None, :, None, None])
        * prev_mask[:, :, None, None]
    )
    convolved = convolved + jnp.einsum(
        "btgm,bgmc->btgc", lead_weight * res_dev[None, None], blk_in, precision=HIGHEST
    )
    mixed = (query_wide * convolved).astype(jnp.bfloat16).reshape(tokens, channels)
    grad_query = (grad_wide * convolved).astype(jnp.bfloat16).reshape(tokens, channels)
    _, blk_out = lax.scan(fold_blocks, carry_out, (blk_back_decay, blk_back), reverse=True)
    next_mask = (docs_blk == blk_after[:, None]).astype(jnp.float32)
    tail_weight = (
        jnp.exp(-rate_dev[None, None] * (BLOCK - lag_float)[None, :, None, None])
        * next_mask[:, :, None, None]
    )
    dmix = dmix + jnp.einsum(
        "bsgm,bgmc->bsgc", tail_weight * res_dev[None, None], blk_out, precision=HIGHEST
    )
    grad_key = (dmix * value_wide).astype(jnp.bfloat16).reshape(tokens, channels)
    grad_value = (dmix * key_wide).astype(jnp.bfloat16).reshape(tokens, channels)
    pairs = jnp.einsum("btgc,bsgc->bgts", dconv, mixture, precision=HIGHEST) * same_doc[:, None]
    growth = jnp.exp(rate_dev[:, :, None] * lag_float)
    partial_sum = jnp.einsum("bgts,gms->bgtm", pairs, growth, precision=HIGHEST)
    grad_local = jnp.einsum("bgtm,gmt->gm", partial_sum, powers, precision=HIGHEST)
    carried = jnp.einsum("btgc,bgmc->btgm", dconv, blk_in, precision=HIGHEST)
    grad_local = grad_local + jnp.sum(carried * lead_weight, axis=(0, 1))
    padded = jnp.zeros((groups_dev * tp_count, MODES), jnp.float32)
    padded = lax.dynamic_update_slice_in_dim(padded, grad_local, tp_pos * groups_dev, 0)
    owned = lax.psum_scatter(padded, ("ctx", "tp"), scatter_dimension=0, tiled=True)
    grad_residues = owned / seq_len
    return (mixed, grad_query, grad_key, grad_value, grad_residues)


def solution(mesh):
    in_specs = (
        P("ctx", "tp"),
        P("ctx", "tp"),
        P("ctx", "tp"),
        P("ctx", "tp"),
        P(("ctx", "tp"), None),
        P(("ctx", "tp"), None),
        P(),
    )
    out_specs = (
        P("ctx", "tp"),
        P("ctx", "tp"),
        P("ctx", "tp"),
        P("ctx", "tp"),
        P(("ctx", "tp"), None),
    )
    return jax.shard_map(
        per_device, mesh=mesh, in_specs=in_specs, out_specs=out_specs, check_vma=False
    )
```

profile of v0, /device:TPU:4, one launch (start us, length us, event | category | flops | bytes accessed | tf_op | source)
XLA Modules:
  0.0 454.3 jit_solution(1562330043333598051)
XLA Ops:
  15.9 1.1 copy.88
  17.1 1.1 copy.89
  18.2 66.2 %all-gather.5 = f32[256,2,16]{2,1,0:T(2,128)S(1)} all-gather(f32[1,2,16]{2,1,0:T(2,128)} %bitcast.123), channel_id=1, replica_groups=mesh['ctx'=32,'tp'=8] {'ctx','tp'}, dimensions={0}, use_global_device_ids=true | all-gather | bytes 32896 | tf_op jit(solution)/shard_map/all_gather | solution.py:50
  84.6 2.6 compare_convert_fusion
  87.3 1.9 convolution_add_fusion.1
  89.7 1.9 convolution_add_fusion
  91.8 8.2 %fusion.75 = f32[64,128,128]{2,1,0:T(8,128)} fusion(f32[128,64,16]{0,2,1:T(8,128)S(1)} %bitcast.103, f32[128,64,16]{0,2,1:T(8,128)S(1)} %bitcast.107), kind=kOutput, calls=%fused_computation.105 | convolution fusion | flops 201326592 | bytes 5242880 | tf_op jit(solution)/shard_map/btgc,bsgc->bgts/dot_general | solution.py:141
  100.0 62.9 %all-gather.4 = f32[256,2,16]{2,1,0:T(2,128)S(1)} all-gather(f32[1,2,16]{2,1,0:T(2,128)S(1)} %bitcast.124), channel_id=1, replica_groups=mesh['ctx'=32,'tp'=8] {'ctx','tp'}, dimensions={0}, use_global_device_ids=true | all-gather | bytes 32896 | tf_op jit(solution)/shard_map/all_gather | solution.py:49
  163.7 24.0 %all-gather.7 = f32[32,64,16]{1,2,0:T(8,128)S(1)} all-gather(f32[1,64,16]{1,2,0:T(8,128)S(1)} %get-tuple-element.356), channel_id=4, replica_groups=mesh['ctx'=32,'tp'=8] {'ctx'}, dimensions={0}, use_global_device_ids=true | all-gather | bytes 135168 | tf_op jit(solution)/shard_map/all_gather | solution.py:16
  188.4 22.9 %all-gather.6 = f32[32,64,16]{1,2,0:T(8,128)S(1)} all-gather(f32[1,64,16]{1,2,0:T(8,128)S(1)} %get-tuple-element.358), channel_id=2, replica_groups=mesh['ctx'=32,'tp'=8] {'ctx'}, dimensions={0}, use_global_device_ids=true | all-gather | bytes 135168 | tf_op jit(solution)/shard_map/all_gather | solution.py:16
  211.3 4.7 %copy_multiply_fusion = f32[64,128,128]{2,0,1:T(8,128)S(1)} fusion(f32[64,128,128]{2,1,0:T(8,128)} %fusion.75, f32[128,128]{1,0:T(8,128)S(1)} %and_convert_fusion), kind=kLoop, calls=%fused_computation.10 | loop fusion | flops 1048576 | bytes 8454144 | tf_op jit(solution)/shard_map/mul | solution.py:141
  216.1 4.6 %fusion.10 = f32[64,128,128]{2,0,1:T(8,128)} fusion(f32[64,128,1]{1,0,2:T(8,128)S(1)} %bitcast.120, s32[128,128]{1,0:T(8,128)S(1)} %iota_subtract_fusion, f32[128,128]{1,0:T(8,128)S(1)} %and_convert_fusion), kind=kOutput, calls=%fused_computation.16 | convolution fusion | flops 1613758464 | bytes 4358144 | tf_op jit(solution)/shard_map/gk,kts->gts/dot_general | solution.py:77
  220.6 8.2 %fusion.27 = f32[64,16]{1,0:T(8,128)S(1)} fusion(f32[64,128,128]{2,0,1:T(8,128)S(1)} %copy_multiply_fusion, f32[64,16]{1,0:T(8,128)S(1)} %copy.102, f32[128]{0:T(128)S(1)} %iota_convert_fusion, f32[64,16]{1,0:T(8,128)S(1)} %copy.91), kind=kOutput, calls=%fused_computation.26 | convolution fusion | flops 201849856 | bytes 4207104 | tf_op jit(solution)/shard_map/bgts,gms->bgtm/dot_general | solution.py:143
  228.9 12.1 %copy.95 = f32[32,64,16,16]{1,3,2,0:T(8,128)} copy(f32[32,64,16,16]{3,2,1,0:T(8,128)} %bitcast.101) | data formatting | bytes 4194304
  241.0 32.2 %while.18 = (s32[]{:T(128)}, f32[64,16,16]{0,2,1:T(8,128)S(1)}, s32[]{:T(128)}, f32[32,64,16]{1,2,0:T(8,128)S(1)}, f32[32,64,16,16]{1,3,2,0:T(8,128)}, /*index=5*/s32[]{:T(128)}, s32[]{:T(128)}) while((s32[]{:T(128)}, f32[64,16,16]{0,2,1:T(8,128)S(1)}, s32[]{:T(128)}, f32[32,64,16]{1,2,0:T(8,128)S(1)}, ...), condition=%wide.region_5.6_spmd.clone, body=%wide.region_4.5_spmd.clone.sunk | while | flops 65540 | bytes 209009 | solution.py:28
  242.0 1.0 fusion.90
  243.0 1.0 fusion.90
  244.1 1.0 fusion.90
  245.1 1.0 fusion.90
  246.2 1.0 fusion.90
  247.2 1.0 fusion.90
  248.2 1.0 fusion.90
  249.3 1.0 fusion.90
  250.3 1.0 fusion.90
  251.4 1.0 fusion.90
  252.4 1.0 fusion.90
  253.4 1.0 fusion.90
  254.5 1.0 fusion.90
  255.5 1.0 fusion.90
  256.6 1.0 fusion.90
  257.6 1.0 fusion.90
  258.6 1.0 fusion.90
  259.7 1.0 fusion.90
  260.7 1.0 fusion.90
  262.8 1.0 fusion.90
  263.8 1.0 fusion.90
  265.9 1.0 fusion.90
  267.0 1.0 fusion.90
  269.1 1.0 fusion.90
  272.2 1.0 fusion.90
  274.3 1.3 fusion.41
  275.6 12.0 %copy.100 = f32[32,64,16,16]{1,3,2,0:T(8,128)} copy(f32[32,64,16,16]{3,2,1,0:T(8,128)} %bitcast.100) | data formatting | bytes 4194304 | tf_op jit(solution)/shard_map/all_gather | solution.py:16
  287.6 4.6 %rev.7 = f32[32,64,16,16]{1,3,2,0:T(8,128)} reverse(f32[32,64,16,16]{1,3,2,0:T(8,128)} %copy.100), dimensions={0} | reverse | bytes 4194304 | tf_op jit(solution)/shard_map/rev | solution.py:18
  292.2 53.4 %while.19 = (s32[]{:T(128)}, f32[64,16,16]{0,2,1:T(8,128)S(1)}, s32[]{:T(128)}, f32[32,64,16]{1,2,0:T(8,128)}, f32[32,64,16,16]{1,3,2,0:T(8,128)}, /*index=5*/s32[]{:T(128)}, s32[]{:T(128)}) while((s32[]{:T(128)}, f32[64,16,16]{0,2,1:T(8,128)S(1)}, s32[]{:T(128)}, f32[32,64,16]{1,2,0:T(8,128)}, f32[32,64,16,16]{1,3,2,0:T(8,128)}, ...), condition=%wide.region_9.10_spmd.clone, body=%wide.region_8.9_spmd.clone.sunk | while | flops 65540 | bytes 209009 | solution.py:28
  345.9 11.3 %multiply_convert_fusion.2 = (bf16[1,128,64,16]{1,3,2,0:T(8,128)(2,1)}, bf16[1,128,64,16]{1,3,2,0:T(8,128)(2,1)S(1)}) fusion(f32[64,16,128]{2,1,0:T(8,128)S(1)} %fusion.41, f32[128,64,16]{0,2,1:T(8,128)S(1)} %bitcast.108, f32[64,128,128]{2,0,1:T(8,128)} %fusion.10, bf16[1,128,64,16]{1,3,2,0:T(8,128)(2,1)S(1)} %bitcast.112, ...), kind=kOutput, calls=%fused_computation.40 | convolution fusion | flops 202244096 | bytes 6291456 | tf_op jit(solution)/shard_map/bgts,bsgc->btgc/dot_general | solution.py:89
  357.2 1.8 copy.108
  360.7 8.2 %multiply_convert_fusion = (bf16[1,128,64,16]{1,3,2,0:T(8,128)(2,1)S(1)}, bf16[1,128,64,16]{1,3,2,0:T(8,128)(2,1)S(1)}) fusion(f32[64,16,128]{2,1,0:T(8,128)S(1)} %fusion.33, f32[128,64,16]{0,2,1:T(8,128)S(1)} %bitcast.105, f32[64,128,128]{2,0,1:T(8,128)} %fusion.10, bf16[1,128,64,16]{1,3,2,0:T(8,128)(2,1)S(1)} %bitcast.109, ...), kind=kOutput, calls=%fused_computation.30 | convolution fusion | flops 202244096 | bytes 6291456 | tf_op jit(solution)/shard_map/bgts,btgc->bsgc/dot_general | solution.py:101
  370.6 76.3 %all-reduce = f32[512,16]{1,0:T(8,128)S(1)} all-reduce(f32[512,16]{1,0:T(8,128)S(1)} %add_dynamic-update-slice_fusion), channel_id=6, replica_groups=mesh['ctx'=32,'tp'=8] {'ctx','tp'}, use_global_device_ids=true, to_apply=%region_11.12.clone | all-reduce | flops 8192 | bytes 65536
  (150 shorter events, 70.3 us)
Async XLA Ops:
  7.2 82.0 %copy-start = (bf16[128,1024]{1,0:T(8,128)(2,1)S(1)}, bf16[128,1024]{1,0:T(8,128)(2,1)}, u32[]{:S(2)}) copy-start(bf16[128,1024]{1,0:T(8,128)(2,1)} %param.11) | copy-start | bytes 786436
  7.2 82.2 %copy-start.1 = (bf16[128,1024]{1,0:T(8,128)(2,1)S(1)}, bf16[128,1024]{1,0:T(8,128)(2,1)}, u32[]{:S(2)}) copy-start(bf16[128,1024]{1,0:T(8,128)(2,1)} %param.14) | copy-start | bytes 786436
  7.2 221.7 %all-gather.11.cloned.1.call-start = ((), (), s32[]{:S(2)}) async-start(), calls=%async_computation | async-start | bytes 17301504 | tf_op jit(solution)/shard_map/all_gather | solution.py:16
  89.2 186.4 %all-gather.13.cloned.1.call-start = ((), (), s32[]{:S(2)}) async-start(), calls=%async_computation.1 | async-start | bytes 17301504 | tf_op jit(solution)/shard_map/all_gather | solution.py:16
  89.6 10.4 %copy-start.2 = (f32[2,16]{1,0:T(2,128)S(1)}, f32[2,16]{1,0:T(2,128)}, u32[]{:S(2)}) copy-start(f32[2,16]{1,0:T(2,128)} %param.15) | copy-start | bytes 388
Sparse Core Ops, SparseCore 0:
  89.3 74.1 all-gather.10
  166.0 77.3 all-gather.12
where the time goes:
time: 460 us; the launch traced here: 454 us
  blocking collectives  252 us (55%)
  other arithmetic  72.4 us (16%)
  local copies, waits for them, and re-layouts  60.5 us (13%)
  matrix products  47.9 us (10%)
  between operations  19.5 us (4%)
    unnamed x1, blocking collectives  76.3 us
    all_gather x1, blocking collectives, per_device(): lax.all_gather(decay_time, ('ctx', 'tp'), axis=0, tiled=True)  66.2 us
    all_gather x1, blocking collectives, per_device(): lax.all_gather(residues, ('ctx', 'tp'), axis=0, tiled=True)  62.9 us
    select_n x62, other arithmetic, lap(): jnp.where(position < mine, new, old)  61.9 us
    all_gather x2, blocking collectives, entering(): pieces = jax.tree.map(lambda part: lax.all_gather(part, axis), value)  46.9 us
    mul x62, local copies, waits for them, and re-layouts, chain(): later_part[0][..., None] * earlier[1] + later_part[1]  22 us
    unnamed x16, local copies, waits for them, and re-layouts  19.1 us
    all_gather x1, local copies, waits for them, and re-layouts, entering(): pieces = jax.tree.map(lambda part: lax.all_gather(part, axis), value)  12 us
  transfers between devices with their start and end apart: 2, of which 0 were waited for; matrix products, arithmetic and copies ran while one was open for 17% of the time, Pallas kernels for 0%

commit v1 on v0

v1 whole, which is shorter than its diff:
```python
import functools

import jax
import jax.numpy as jnp
from jax import lax
from jax.experimental import pallas as pl
from jax.experimental.pallas import tpu as pltpu
from jax.sharding import PartitionSpec as P

GROUP = 16
MODES = 16
LANES = 128
TILE_GROUPS = LANES // GROUP
OWN_GROUPS = 2
PIECES = TILE_GROUPS // OWN_GROUPS
ROWS = GROUP // PIECES

F32 = jnp.float32
BF16 = jnp.bfloat16
MESH = pl.DeviceIdType.MESH


def halves(x):
    high = x.astype(BF16)
    return high, (x - high.astype(F32)).astype(BF16)


def wide(x):
    return jnp.concatenate(halves(x), axis=1)


def fold(product):
    return product[:, :LANES] + product[:, LANES:]


def twice(x):
    return jnp.concatenate([x, x], axis=0)


def dot_wide(left, right):
    return fold(jnp.dot(left, twice(right), preferred_element_type=F32))


def dot_wide_nt(left, high, low):
    right = jnp.concatenate(
        [jnp.concatenate([high, high], axis=1), jnp.concatenate([low, low], axis=1)], axis=0
    )
    product = lax.dot_general(left, right, (((1,), (1,)), ((), ())), preferred_element_type=F32)
    return fold(product)


def iota(shape, dim):
    return lax.broadcasted_iota(jnp.int32, shape, dim)


def exchange_kernel(
    nctx,
    ntp,
    doc_ref,
    query_hbm,
    key_hbm,
    value_hbm,
    grad_hbm,
    res_hbm,
    time_hbm,
    conv_ref,
    dmix_ref,
    grad_res_ref,
    query,
    key,
    value,
    grad,
    res,
    time,
    par_send,
    par_recv,
    mix_wide,
    dconv_wide,
    mix_t,
    dconv_t,
    lead_wide,
    tail_wide,
    decay_wide,
    flip_wide,
    state_send,
    state_recv,
    carry_send,
    carry_recv,
    corr_send,
    corr_recv,
    part_send,
    part_recv,
    load_sem,
    send_sem,
    recv_sem,
):
    tokens, channels = query.shape
    tiles = channels // LANES
    seq_len = tokens * nctx
    c = lax.axis_index("ctx")
    p = lax.axis_index("tp")
    flat = c * ntp + p
    plane = flat // nctx
    mine = lax.rem(flat, nctx)
    owns_here = plane == p

    def owner(block):
        device = p * nctx + block
        return device // ntp, lax.rem(device, ntp)

    def push(src, dst, kind, ctx_to, tp_to):
        here = jnp.logical_and(ctx_to == c, tp_to == p)

        @pl.when(jnp.logical_not(here))
        def _():
            pltpu.make_async_remote_copy(
                src_ref=src,
                dst_ref=dst,
                send_sem=send_sem.at[kind],
                recv_sem=recv_sem.at[kind],
                device_id=(ctx_to, tp_to),
                device_id_type=MESH,
            ).start()

        @pl.when(here)
        def _():
            pltpu.make_async_copy(src, dst, recv_sem.at[kind]).start()

    def arrived(ref, kind):
        pltpu.make_async_copy(ref, ref, recv_sem.at[kind]).wait()

    def sent(ref, kind):
        pltpu.make_async_copy(ref, ref, send_sem.at[kind]).wait()

    sources = (query_hbm, key_hbm, value_hbm, grad_hbm, res_hbm, time_hbm)
    targets = (query, key, value, grad, res, time)
    loads = [
        pltpu.make_async_copy(src, dst, load_sem.at[i])
        for i, (src, dst) in enumerate(zip(sources, targets))
    ]
    for i in (4, 5, 1, 2, 0, 3):
        loads[i].start()

    barrier = pltpu.get_barrier_semaphore()

    def greet(i, _):
        block = lax.rem(mine + i, nctx)
        ctx_to, tp_to = owner(block)

        @pl.when(jnp.logical_not(jnp.logical_and(ctx_to == c, tp_to == p)))
        def _():
            pl.semaphore_signal(
                barrier, inc=1, device_id=(ctx_to, tp_to), device_id_type=MESH
            )

        return 0

    lax.fori_loop(0, nctx, greet, 0)

    loads[4].wait()
    loads[5].wait()
    rate = 1.0 / time[...]
    residue = res[...]
    par_send[0:1, :] = jnp.concatenate([rate[0:1], rate[1:2]] * PIECES, axis=1)
    par_send[1:2, :] = jnp.concatenate([residue[0:1], residue[1:2]] * PIECES, axis=1)

    @pl.when(owns_here)
    def _():
        pl.semaphore_wait(barrier, nctx - 1)

    @pl.when(jnp.logical_not(owns_here))
    def _():
        pl.semaphore_wait(barrier, nctx)

    def send_par(i, _):
        push(par_send, par_recv.at[mine], 0, lax.rem(c + i, nctx), plane)
        return 0

    lax.fori_loop(0, nctx, send_par, 0)

    first = c * tokens
    end0 = doc_ref[0]
    end1 = end0 + doc_ref[1]
    end2 = end1 + doc_ref[2]
    end3 = end2 + doc_ref[3]
    ends = (end0, end1, end2, end3)

    def doc_of(position):
        total = (position >= end0).astype(jnp.int32)
        for end in ends[1:]:
            total = total + (position >= end).astype(jnp.int32)
        return total

    square = (tokens, LANES)
    row = iota(square, 0)
    col = iota(square, 1)
    doc_row = doc_of(first + row)
    doc_col = doc_of(first + col)
    same = doc_row == doc_col
    upper = jnp.where(jnp.logical_and(same, col >= row), 1.0, 0.0)
    lower = jnp.where(jnp.logical_and(same, col <= row), 1.0, 0.0)
    flip_row = tokens - 1 - row
    turned = jnp.where(
        jnp.logical_and(doc_of(first + flip_row) == doc_col, col >= flip_row), 1.0, 0.0
    )
    turn = jnp.where(flip_row == col, 1.0, 0.0).astype(BF16)
    block_of = iota((1, LANES), 1) // GROUP

    for i in (1, 2, 0, 3):
        loads[i].wait()

    def lanes_of(q):
        return pl.ds(pl.multiple_of(q * LANES, LANES), LANES)

    def local(q, _):
        at = lanes_of(q)
        mixture = key[:, at].astype(F32) * value[:, at].astype(F32)
        dconv = grad[:, at].astype(F32) * query[:, at].astype(F32)
        mix_high, mix_low = halves(mixture)
        d_high, d_low = halves(dconv)
        mix_wide[q] = jnp.concatenate([mix_high, mix_low], axis=1)
        dconv_wide[q] = jnp.concatenate([d_high, d_low], axis=1)
        mix_t[q] = wide(mixture.T)
        dconv_t[q] = wide(dconv.T)
        right = jnp.concatenate(
            [jnp.concatenate([d_high, d_high], axis=1), jnp.concatenate([d_low, d_low], axis=1)],
            axis=0,
        )
        left = jnp.dot(
            turn, jnp.concatenate([mix_high, mix_low], axis=1), preferred_element_type=F32
        ).astype(BF16)
        lane_block = lax.rem(iota((1, 2 * LANES), 1), LANES) // GROUP
        for g in range(TILE_GROUPS):
            masked = jnp.where(lane_block == g, left, jnp.zeros_like(left))
            pairs = fold(
                lax.dot_general(masked, right, (((1,), (1,)), ((), ())), preferred_element_type=F32)
            )
            lags = pltpu.roll(pairs * turned, 1, 1, stride=1, stride_axis=0)
            corr_send[PIECES * q + g // OWN_GROUPS, g % OWN_GROUPS : g % OWN_GROUPS + 1, :] = (
                jnp.sum(lags, axis=0, keepdims=True)
            )
        return 0

    lax.fori_loop(0, tiles, local, 0)

    arrived(par_recv, 0)

    def par_row(q, which):
        lane_piece = iota((1, LANES), 1) // (LANES // PIECES)
        out = par_recv[PIECES * q, which : which + 1, :]
        for b in range(1, PIECES):
            out = jnp.where(lane_piece == b, par_recv[PIECES * q + b, which : which + 1, :], out)
        return out

    pos = row.astype(F32)
    doc_first = doc_of(first)
    doc_last = doc_of(first + tokens - 1)
    doc_before = doc_of(first - 1)
    doc_after = doc_of(first + tokens)
    at_start = jnp.where(doc_row == doc_first, 1.0, 0.0)
    at_end = jnp.where(doc_row == doc_last, 1.0, 0.0)
    with_before = jnp.where(doc_row == doc_before, 1.0, 0.0)
    with_after = jnp.where(doc_row == doc_after, 1.0, 0.0)

    def own_blocks(x):
        out = jnp.zeros((GROUP, LANES), F32)
        for g in range(TILE_GROUPS):
            out = jnp.where(block_of == g, x[g * GROUP : (g + 1) * GROUP, :], out)
        return out

    def states(step, _):
        q = lax.rem(c // PIECES + step, tiles)
        rate_row = par_row(q, 0)
        decay = jnp.exp(-pos * rate_row)
        flip = jnp.exp((pos - (tokens - 1.0)) * rate_row)
        decay_wide[q] = wide(decay)
        flip_wide[q] = wide(flip)
        end_state = own_blocks(dot_wide(mix_t[q], wide(flip * at_end)))
        start_state = own_blocks(dot_wide(dconv_t[q], wide(decay * at_start)))
        for r in range(PIECES):
            j = PIECES * q + r
            state_send[j, 0:ROWS, :] = end_state[r * ROWS : (r + 1) * ROWS, :]
            state_send[j, ROWS:, :] = start_state[r * ROWS : (r + 1) * ROWS, :]
            push(state_send.at[j], state_recv.at[c], 1, j, p)
        return 0

    lax.fori_loop(0, tiles, states, 0)

    def send_corr(i, _):
        block = lax.rem(mine + i, nctx)
        ctx_to, tp_to = owner(block)
        push(corr_send.at[block], corr_recv.at[c], 2, ctx_to, tp_to)
        return 0

    lax.fori_loop(0, nctx, send_corr, 0)

    def selected(q):
        res_row = par_row(q, 1)
        chosen = jnp.where(block_of == iota((TILE_GROUPS, LANES), 0), res_row, 0.0)
        return res_row, wide(chosen)

    def conv_local(q, _):
        rate_row = par_row(q, 0)
        res_row, chosen = selected(q)
        flip = flip_wide[q]
        taps = dot_wide_nt(chosen, flip[:, :LANES], flip[:, LANES:])
        right = mix_wide[q]
        total = jnp.zeros(square, F32)
        for g in range(TILE_GROUPS):
            spread = jnp.broadcast_to(taps[g : g + 1, :], square)
            toeplitz = pltpu.roll(spread, 1, 1, stride=1, stride_axis=0) * lower
            total = jnp.where(block_of == g, dot_wide(wide(toeplitz), right), total)
        conv_ref[:, lanes_of(q)] = total
        lead_wide[q] = wide(jnp.exp(-(pos + 1.0) * rate_row) * (res_row * with_before))
        return 0

    lax.fori_loop(0, tiles, conv_local, 0)

    arrived(state_recv, 1)
    my_rate = par_row(c // PIECES, 0)
    span = jnp.exp(-float(tokens) * my_rate)
    once = jnp.exp(-my_rate)
    piece = (2 * ROWS, LANES)
    cut_in = [jnp.full(piece, end // tokens, jnp.int32) for end in ends[:3]]
    cut_out = [jnp.full(piece, (end - 1) // tokens, jnp.int32) for end in ends[:3]]
    cut_at = [jnp.full(piece, end, jnp.int32) for end in ends[:3]]
    is_end = iota(piece, 0) < ROWS

    def kept(cuts, at, factor):
        hit = cuts[0] == at
        for cut in cuts[1:]:
            hit = jnp.logical_or(hit, cut == at)
        return jnp.where(hit, 0.0, factor)

    back = jnp.zeros(piece, F32)
    for i in range(nctx - 1, -1, -1):
        carry_send[i] = back
        back = kept(cut_out, i, span) * back + state_recv[i]
    ahead = jnp.zeros(piece, F32)
    carried = jnp.zeros(piece, F32)
    for i in range(nctx):
        here = state_recv[i]
        carry_send[i] = jnp.where(is_end, ahead, carry_send[i])
        push(carry_send.at[i], carry_recv.at[c], 3, i, p)
        begun = pltpu.roll(here, ROWS, 0)
        carried = carried + kept(cut_at, i * tokens, once) * (ahead * begun)
        ahead = kept(cut_in, i, span) * ahead + here
    carried = jnp.where(is_end, carried, 0.0)
    part_send[...] = jnp.sum(carried, axis=0, keepdims=True)
    for b in range(PIECES):
        block = (c // PIECES) * PIECES + b
        ctx_to, tp_to = owner(block)
        push(part_send, part_recv.at[lax.rem(c, PIECES)], 4, ctx_to, tp_to)

    def dmix_local(q, _):
        rate_row = par_row(q, 0)
        res_row, chosen = selected(q)
        decay = decay_wide[q]
        taps = dot_wide_nt(chosen, decay[:, :LANES], decay[:, LANES:])
        right = dconv_wide[q]
        total = jnp.zeros(square, F32)
        for g in range(TILE_GROUPS):
            spread = jnp.broadcast_to(taps[g : g + 1, :], square)
            toeplitz = pltpu.roll(spread, 0, 1, stride=1, stride_axis=0) * upper
            total = jnp.where(block_of == g, dot_wide(wide(toeplitz), right), total)
        dmix_ref[:, lanes_of(q)] = total
        tail_wide[q] = wide(jnp.exp((pos - float(tokens)) * rate_row) * (res_row * with_after))
        return 0

    lax.fori_loop(0, tiles, dmix_local, 0)

    arrived(corr_recv, 2)

    def add_corr(i, total):
        return total + corr_recv[i]

    corr = lax.fori_loop(0, nctx, add_corr, jnp.zeros((OWN_GROUPS, LANES), F32))
    powers = jnp.exp(-pos * par_send[0:1, :])
    by_mode = dot_wide(wide(jnp.concatenate([corr] * PIECES, axis=0)), wide(powers))
    lane = iota((1, LANES), 1)
    grad_row = jnp.where(lax.rem(lane // MODES, OWN_GROUPS) == 0, by_mode[0:1], by_mode[1:2])
    arrived(part_recv, 4)
    for r in range(PIECES):
        grad_row = grad_row + part_recv[r]
    step = LANES // PIECES
    grad_row = jnp.where(lane // step == lax.rem(mine, PIECES), grad_row / seq_len, 0.0)
    whole = grad_row
    for b in range(1, PIECES):
        whole = whole + pltpu.roll(grad_row, b * step, 1)
    grad_res_ref[0:1, :] = whole[:, :MODES]
    grad_res_ref[1:2, :] = pltpu.roll(whole, LANES - MODES, 1)[:, :MODES]

    arrived(carry_recv, 3)
    own = iota((LANES, LANES), 0) // GROUP == iota((LANES, LANES), 1) // MODES

    def spread_out(q, rows):
        state = jnp.concatenate(
            [carry_recv[PIECES * q + r, rows, :] for r in range(PIECES)], axis=0
        )
        state = jnp.where(own, jnp.concatenate([state] * TILE_GROUPS, axis=0), 0.0)
        return halves(state)

    def enter(q, _):
        at = lanes_of(q)
        conv_ref[:, at] += dot_wide_nt(lead_wide[q], *spread_out(q, slice(0, ROWS)))
        dmix_ref[:, at] += dot_wide_nt(tail_wide[q], *spread_out(q, slice(ROWS, 2 * ROWS)))
        return 0

    lax.fori_loop(0, tiles, enter, 0)

    sent(state_send.at[pl.ds(0, nctx - 1)], 1)
    sent(carry_send.at[pl.ds(0, nctx - 1)], 3)

    @pl.when(owns_here)
    def _():
        sent(par_recv.at[pl.ds(0, nctx - 1)], 0)
        sent(corr_send.at[pl.ds(0, nctx - 1)], 2)

    @pl.when(jnp.logical_not(owns_here))
    def _():
        sent(par_recv, 0)
        sent(corr_send, 2)

    to_self = jnp.logical_and(owns_here, mine // PIECES == c // PIECES)

    @pl.when(to_self)
    def _():
        sent(part_recv.at[pl.ds(0, PIECES - 1)], 4)

    @pl.when(jnp.logical_not(to_self))
    def _():
        sent(part_recv, 4)


def per_device(nctx, ntp, query, key, value, grad, residues, decay_time, doc_lengths):
    tokens, channels = query.shape
    tiles = channels // LANES
    vmem = pl.BlockSpec(memory_space=pltpu.VMEM)
    hbm = pl.BlockSpec(memory_space=pl.ANY)
    flat = jax.ShapeDtypeStruct((tokens, channels), F32)
    pair = pltpu.VMEM((tiles, LANES, 2 * LANES), BF16)
    piece = pltpu.VMEM((nctx, 2 * ROWS, LANES), F32)
    conv, dmix, grad_res = pl.pallas_call(
        functools.partial(exchange_kernel, nctx, ntp),
        out_shape=(flat, flat, jax.ShapeDtypeStruct(residues.shape, F32)),
        in_specs=[pl.BlockSpec(memory_space=pltpu.SMEM)] + [hbm] * 6,
        out_specs=(vmem, vmem, vmem),
        scratch_shapes=[pltpu.VMEM((tokens, channels), BF16)] * 4
        + [pltpu.VMEM((OWN_GROUPS, MODES), F32)] * 2
        + [pltpu.VMEM((OWN_GROUPS, LANES), F32), pltpu.VMEM((nctx, OWN_GROUPS, LANES), F32)]
        + [pair] * 8
        + [piece] * 4
        + [pltpu.VMEM((nctx, OWN_GROUPS, LANES), F32)] * 2
        + [pltpu.VMEM((1, LANES), F32), pltpu.VMEM((PIECES, 1, LANES), F32)]
        + [
            pltpu.SemaphoreType.DMA((6,)),
            pltpu.SemaphoreType.DMA((5,)),
            pltpu.SemaphoreType.DMA((5,)),
        ],
        compiler_params=pltpu.CompilerParams(
            collective_id=0, has_side_effects=True, vmem_limit_bytes=48 * 1024 * 1024
        ),
    )(doc_lengths, query, key, value, grad, residues, decay_time)
    mixed = (query.astype(F32) * conv).astype(BF16)
    grad_query = (grad.astype(F32) * conv).astype(BF16)
    grad_key = (dmix * value.astype(F32)).astype(BF16)
    grad_value = (dmix * key.astype(F32)).astype(BF16)
    return mixed, grad_query, grad_key, grad_value, grad_res


def solution(mesh):
    main = P("ctx", "tp")
    owned = P(("ctx", "tp"), None)
    return jax.shard_map(
        functools.partial(per_device, mesh.shape["ctx"], mesh.shape["tp"]),
        mesh=mesh,
        in_specs=(main, main, main, main, owned, owned, P()),
        out_specs=(main, main, main, main, owned),
        check_vma=False,
    )
```

time: 460 us -> 42.9 us (0.09); the launches traced: 454 us -> 42.7 us
  blocking collectives: 252 us -> 0 us
  other arithmetic: 72.4 us -> 1.2 us
  local copies, waits for them, and re-layouts: 60.5 us -> 6.37 us
  matrix products: 47.9 us -> 0 us
  Pallas kernels: 0 us -> 34.5 us
  between operations: 19.5 us -> 0.66 us
    all_gather x4 -> x0, blocking collectives: 176 us -> none  [the longest x1 66.2 us: per_device(): lax.all_gather(decay_time, ('ctx', 'tp'), axis=0, tiled=True)]
    unnamed x1 -> x0, blocking collectives: 76.3 us -> none
    select_n x62 -> x0, other arithmetic: 61.9 us -> none  [lap(): jnp.where(position < mine, new, old)]
    dot_general x11 -> x0, matrix products: 47.9 us -> none  [the longest x1 11.3 us: per_device(): jnp.einsum('bgts,bsgc->btgc', kernel, mixture, precision=HIGHEST)]
    pallas_call x0 -> x1, Pallas kernels: none -> 34.5 us  [per_device(): pl.pallas_call(functools.partial(exchange_kernel, nctx, ntp), out_shape=(...]
    mul x64 -> x0, local copies, waits for them, and re-layouts: 22.2 us -> none  [the longest x62 22 us: chain(): later_part[0][..., None] * earlier[1] + later_part[1]]
    unnamed x16 -> x15, local copies, waits for them, and re-layouts: 19.1 us -> 6.37 us
    all_gather x1 -> x0, local copies, waits for them, and re-layouts: 12 us -> none  [entering(): pieces = jax.tree.map(lambda part: lax.all_gather(part, axis), value)]
  transfers between devices with their start and end apart: 2 -> 0, of which waited for: 0 -> 0; matrix products, arithmetic and copies ran while one was open for 17% -> 0% of each run, Pallas kernels for 0% -> 0%
where the time goes in v1:
time: 42.9 us; the launch traced here: 42.7 us
  Pallas kernels  34.5 us (80%)
  local copies, waits for them, and re-layouts  6.37 us (15%)
  other arithmetic  1.2 us (3%)
  between operations  0.66 us (2%)
    pallas_call x1, Pallas kernels, per_device(): pl.pallas_call(functools.partial(exchange_kernel, nctx, ntp), out_shape=(...  34.5 us
    unnamed x15, local copies, waits for them, and re-layouts  6.37 us
    convert_element_type x1, other arithmetic, per_device(): grad_value = (dmix * key.astype(F32)).astype(BF16)  1.2 us

profile of v1, /device:TPU:4, one launch (start us, length us, event | category | flops | bytes accessed | tf_op | source)
XLA Modules:
  0.0 42.7 jit_solution(8427089604930610672)
XLA Ops:
  0.6 0.0 copy-start
  0.6 0.9 %copy-done = bf16[128,1024]{1,0:T(8,128)(2,1)S(1)} copy-done((bf16[128,1024]{1,0:T(8,128)(2,1)S(1)}, bf16[128,1024]{1,0:T(8,128)(2,1)}, u32[]{:S(2)}) %copy-start) | copy-done | bytes 262168
  1.6 0.0 copy-start.1
  1.6 0.9 %copy-done.1 = bf16[128,1024]{1,0:T(8,128)(2,1)S(1)} copy-done((bf16[128,1024]{1,0:T(8,128)(2,1)S(1)}, bf16[128,1024]{1,0:T(8,128)(2,1)}, u32[]{:S(2)}) %copy-start.1) | copy-done | bytes 262168
  2.5 0.0 copy-start.2
  2.5 0.9 %copy-done.2 = bf16[128,1024]{1,0:T(8,128)(2,1)S(1)} copy-done((bf16[128,1024]{1,0:T(8,128)(2,1)S(1)}, bf16[128,1024]{1,0:T(8,128)(2,1)}, u32[]{:S(2)}) %copy-start.2) | copy-done | bytes 262168
  3.5 0.0 copy-start.3
  3.5 0.9 %copy-done.3 = bf16[128,1024]{1,0:T(8,128)(2,1)S(1)} copy-done((bf16[128,1024]{1,0:T(8,128)(2,1)S(1)}, bf16[128,1024]{1,0:T(8,128)(2,1)}, u32[]{:S(2)}) %copy-start.3) | copy-done | bytes 262168
  4.4 0.0 copy-start.4
  4.4 0.7 %copy-done.4 = f32[2,16]{1,0:T(2,128)S(1)} copy-done((f32[2,16]{1,0:T(2,128)S(1)}, f32[2,16]{1,0:T(2,128)}, u32[]{:S(2)}) %copy-start.4) | copy-done | bytes 152
  5.1 0.0 copy-start.5
  5.1 0.7 %copy-done.5 = f32[2,16]{1,0:T(2,128)S(1)} copy-done((f32[2,16]{1,0:T(2,128)S(1)}, f32[2,16]{1,0:T(2,128)}, u32[]{:S(2)}) %copy-start.5) | copy-done | bytes 152
  5.8 0.0 copy-start.6
  5.8 0.7 %copy-done.6 = s32[4]{0:T(128)S(1)} copy-done((s32[4]{0:T(128)S(1)}, s32[4]{0:T(128)}, u32[]{:S(2)}) %copy-start.6) | copy-done | bytes 40
  6.5 34.5 %shard_map.110 = (f32[128,1024]{1,0:T(8,128)S(1)}, f32[128,1024]{1,0:T(8,128)S(1)}, f32[2,16]{1,0:T(2,128)S(1)}) custom-call(s32[4]{0:T(128)S(1)} %copy-done.6, bf16[128,1024]{1,0:T(8,128)(2,1)S(1)} %copy-done, bf16[128,1024]{1,0:T(8,128)(2,1)S(1)} %copy-done.1, bf16[128,1024]{1,0:T(8,128)(2,1)S(1)} %copy-done.2, bf16[128,1024]{1,0:T(8,128)(2,1)S(1)} %copy-done.3, ...), custom_call_target="tpu_custom_call" | custom-call | tf_op jit(solution)/shard_map/pallas_call | solution.py:443
  40.9 1.2 %multiply_convert_fusion = (bf16[128,1024]{1,0:T(8,128)(2,1)}, bf16[128,1024]{1,0:T(8,128)(2,1)}, bf16[128,1024]{1,0:T(8,128)(2,1)}, bf16[128,1024]{1,0:T(8,128)(2,1)}) fusion(f32[128,1024]{1,0:T(8,128)S(1)} %get-tuple-element.9, bf16[128,1024]{1,0:T(8,128)(2,1)S(1)} %copy-done.1, bf16[128,1024]{1,0:T(8,128)(2,1)S(1)} %copy-done.2, ...), kind=kLoop, calls=%fused_computation | loop fusion | flops 1572864 | bytes 3145728 | tf_op jit(solution)/shard_map/convert_element_type | solution.py:467
  42.1 0.6 %copy.13 = f32[2,16]{1,0:T(2,128)} copy(f32[2,16]{1,0:T(2,128)S(1)} %get-tuple-element.26) | data formatting | bytes 256
Async XLA Ops:
  0.6 1.0 %copy-start = (bf16[128,1024]{1,0:T(8,128)(2,1)S(1)}, bf16[128,1024]{1,0:T(8,128)(2,1)}, u32[]{:S(2)}) copy-start(bf16[128,1024]{1,0:T(8,128)(2,1)} %query_hbm.1) | copy-start | bytes 786436
  1.6 0.9 %copy-start.1 = (bf16[128,1024]{1,0:T(8,128)(2,1)S(1)}, bf16[128,1024]{1,0:T(8,128)(2,1)}, u32[]{:S(2)}) copy-start(bf16[128,1024]{1,0:T(8,128)(2,1)} %key_hbm.1) | copy-start | bytes 786436
  2.5 0.9 %copy-start.2 = (bf16[128,1024]{1,0:T(8,128)(2,1)S(1)}, bf16[128,1024]{1,0:T(8,128)(2,1)}, u32[]{:S(2)}) copy-start(bf16[128,1024]{1,0:T(8,128)(2,1)} %value_hbm.1) | copy-start | bytes 786436
  3.5 0.9 %copy-start.3 = (bf16[128,1024]{1,0:T(8,128)(2,1)S(1)}, bf16[128,1024]{1,0:T(8,128)(2,1)}, u32[]{:S(2)}) copy-start(bf16[128,1024]{1,0:T(8,128)(2,1)} %grad_hbm.1) | copy-start | bytes 786436
  4.4 0.7 %copy-start.4 = (f32[2,16]{1,0:T(2,128)S(1)}, f32[2,16]{1,0:T(2,128)}, u32[]{:S(2)}) copy-start(f32[2,16]{1,0:T(2,128)} %res_hbm.1) | copy-start | bytes 388
  5.1 0.7 %copy-start.5 = (f32[2,16]{1,0:T(2,128)S(1)}, f32[2,16]{1,0:T(2,128)}, u32[]{:S(2)}) copy-start(f32[2,16]{1,0:T(2,128)} %time_hbm.1) | copy-start | bytes 388
  5.8 0.7 %copy-start.6 = (s32[4]{0:T(128)S(1)}, s32[4]{0:T(128)}, u32[]{:S(2)}) copy-start(s32[4]{0:T(128)} %doc_ref.1) | copy-start | bytes 52

commit v2 on v1

v2 whole, which is shorter than its diff:
```python
import functools

import jax
import jax.numpy as jnp
from jax import lax
from jax.experimental import pallas as pl
from jax.experimental.pallas import tpu as pltpu
from jax.sharding import PartitionSpec as P

GROUP = 16
MODES = 16
LANES = 128
SUB = 8
TILE_GROUPS = LANES // GROUP
OWN_GROUPS = 2
PIECES = TILE_GROUPS // OWN_GROUPS
ROWS = GROUP // PIECES

F32 = jnp.float32
BF16 = jnp.bfloat16
MESH = pl.DeviceIdType.MESH

PAR, STATE, CORR, CARRY, PART = range(5)


def halves(x):
    high = x.astype(BF16)
    return high, (x - high.astype(F32)).astype(BF16)


def wide(x):
    return jnp.concatenate(halves(x), axis=1)


def fold(product):
    return product[:, :LANES] + product[:, LANES:]


def twice(x):
    return jnp.concatenate([x, x], axis=0)


def dot(left, right):
    return jnp.dot(left, right, preferred_element_type=F32)


def dot_nt(left, right):
    return lax.dot_general(left, right, (((1,), (1,)), ((), ())), preferred_element_type=F32)


def iota(shape, dim):
    return lax.broadcasted_iota(jnp.int32, shape, dim)


def stack_halves(x):
    high, low = halves(x)
    parts = []
    for g in range(TILE_GROUPS):
        rows = slice(g * GROUP, (g + 1) * GROUP)
        parts += [high[rows], low[rows]]
    return jnp.concatenate(parts, axis=0)


def grid_of(nctx):
    chips = nctx // 2
    nx = 1
    while nx * nx * 4 <= chips:
        nx *= 2
    return nx, chips // nx


def far_first(n):
    return sorted(range(n), key=lambda d: -min(d, n - d))


def exchange_kernel(
    nctx,
    ntp,
    doc_hbm,
    query_hbm,
    key_hbm,
    value_hbm,
    grad_hbm,
    res_hbm,
    time_hbm,
    mixed_hbm,
    grad_query_hbm,
    grad_key_hbm,
    grad_value_hbm,
    grad_res_ref,
    doc_ref,
    query,
    key,
    value,
    grad,
    mixed,
    grad_query,
    grad_key,
    grad_value,
    raw,
    par_send,
    par_recv,
    rates,
    weights,
    own_par,
    mix_t,
    dconv_t,
    lead_wide,
    tail_wide,
    conv_t,
    dmix_t,
    state_send,
    state_recv,
    carry_send,
    carry_recv,
    corr_send,
    corr_recv,
    part_send,
    part_recv,
    load_sem,
    store_sem,
    raw_send_sem,
    raw_recv_sem,
    par_recv_sem,
    send_sem,
    recv_sem,
):
    tokens, channels = query.shape
    tiles = channels // LANES
    seq_len = tokens * nctx
    relays = nctx // ntp
    relay_tiles = tiles // relays
    nx, ny = grid_of(nctx)
    c = lax.axis_index("ctx")
    p = lax.axis_index("tp")
    plane = c // relays
    is_relay = plane == p
    mine = lax.rem(c, relays) * ntp + p
    piece_of = lax.rem(c, PIECES)
    tile_of = c // PIECES
    my_x = c // (2 * ny)
    my_y = lax.rem(c // 2, ny)
    my_core = lax.rem(c, 2)

    def remote(src, dst, send, recv, ctx_to, tp_to):
        return pltpu.make_async_remote_copy(
            src_ref=src,
            dst_ref=dst,
            send_sem=send,
            recv_sem=recv,
            device_id=(ctx_to, tp_to),
            device_id_type=MESH,
        )

    def push(src, dst, kind, ctx_to, tp_to):
        here = jnp.logical_and(ctx_to == c, tp_to == p)

        @pl.when(jnp.logical_not(here))
        def _():
            remote(src, dst, send_sem.at[kind], recv_sem.at[kind], ctx_to, tp_to).start()

        @pl.when(here)
        def _():
            pltpu.make_async_copy(src, dst, recv_sem.at[kind]).start()

    def arrived(ref, kind):
        pltpu.make_async_copy(ref, ref, recv_sem.at[kind]).wait()

    def sent(ref, kind):
        pltpu.make_async_copy(ref, ref, send_sem.at[kind]).wait()

    xs = [lax.rem(my_x + d, nx) * (2 * ny) for d in range(nx)]
    ys = [lax.rem(my_y + d, ny) * 2 for d in range(ny)]
    cores = [my_core, 1 - my_core]
    offsets = [(dx, dy, dk) for dx in range(nx) for dy in range(ny) for dk in range(2)]
    offsets.sort(key=lambda o: -(min(o[0], nx - o[0]) + min(o[1], ny - o[1]) + 0.1 * o[2]))
    around = [xs[dx] + ys[dy] + cores[dk] for dx, dy, dk in offsets if dx or dy or dk]

    barrier = pltpu.get_barrier_semaphore()

    def greet(ctx_to, tp_to):
        pl.semaphore_signal(barrier, inc=1, device_id=(ctx_to, tp_to), device_id_type=MESH)

    @pl.when(is_relay)
    def _():
        for d in far_first(ntp):
            if d:
                greet(c, lax.rem(p + d, ntp))

    for a in range(relays):
        relay = p * relays + a

        @pl.when(relay != c)
        def _():
            greet(relay, p)

    sources = (query_hbm, key_hbm, value_hbm, grad_hbm, doc_hbm, time_hbm, res_hbm)
    targets = (query, key, value, grad, doc_ref, own_par.at[0], own_par.at[1])
    loads = [
        pltpu.make_async_copy(src, dst, load_sem.at[i])
        for i, (src, dst) in enumerate(zip(sources, targets))
    ]
    for i in (4, 1, 2, 0, 3, 5, 6):
        loads[i].start()

    def send_raw():
        pl.semaphore_wait(barrier, 1)
        for k, src in enumerate((time_hbm, res_hbm)):
            remote(
                src, raw.at[k, p], raw_send_sem.at[k], raw_recv_sem.at[k, p], c, plane
            ).start()

    @pl.when(p > plane)
    def _():
        send_raw()

    @pl.when(is_relay)
    def _():
        for k, src in enumerate((time_hbm, res_hbm)):
            pltpu.make_async_copy(src, raw.at[k, p], raw_recv_sem.at[k, p]).start()

    first = c * tokens
    loads[4].wait()
    end0 = doc_ref[0]
    end1 = end0 + doc_ref[1]
    end2 = end1 + doc_ref[2]
    end3 = end2 + doc_ref[3]
    ends = (end0, end1, end2, end3)

    def doc_of(position):
        total = (position >= end0).astype(jnp.int32)
        for end in ends[1:]:
            total = total + (position >= end).astype(jnp.int32)
        return total

    square = (tokens, LANES)
    row = iota(square, 0)
    col = iota(square, 1)
    doc_row = doc_of(first + row)
    doc_col = doc_of(first + col)
    flip_row = tokens - 1 - row
    turned = jnp.where(
        jnp.logical_and(doc_of(first + flip_row) == doc_col, col >= flip_row), 1.0, 0.0
    )
    turn = jnp.where(flip_row == col, 1.0, 0.0).astype(BF16)
    block_of = iota((1, LANES), 1) // GROUP

    for i in range(4):
        loads[i].wait()

    def lanes_of(q):
        return pl.ds(pl.multiple_of(q * LANES, LANES), LANES)

    def local(q, _):
        at = lanes_of(q)
        mixture = key[:, at].astype(F32) * value[:, at].astype(F32)
        dconv = grad[:, at].astype(F32) * query[:, at].astype(F32)
        mix_t[q] = stack_halves(mixture.T)
        dconv_t[q] = stack_halves(dconv.T)
        d_high, d_low = halves(dconv)
        right = jnp.concatenate(
            [jnp.concatenate([d_high, d_high], axis=1), jnp.concatenate([d_low, d_low], axis=1)],
            axis=0,
        )
        left = dot(turn, wide(mixture)).astype(BF16)
        lane_block = lax.rem(iota((1, 2 * LANES), 1), LANES) // GROUP
        for g in range(TILE_GROUPS):
            masked = jnp.where(lane_block == g, left, jnp.zeros_like(left))
            lags = pltpu.roll(
                fold(dot_nt(masked, right)) * turned, 1, 1, stride=1, stride_axis=0
            )
            corr_send[PIECES * q + g // OWN_GROUPS, g % OWN_GROUPS : g % OWN_GROUPS + 1, :] = (
                jnp.sum(lags, axis=0, keepdims=True)
            )
        return 0

    lax.fori_loop(0, tiles, local, 0)

    @pl.when(p < plane)
    def _():
        send_raw()

    my_relay = lax.rem(c, relays)

    @pl.when(is_relay)
    def _():
        for k, src in enumerate((time_hbm, res_hbm)):
            for z in range(ntp):
                pltpu.make_async_copy(src, raw.at[k, z], raw_recv_sem.at[k, z]).wait()
        for t in range(relay_tiles):
            for k in range(2):
                parts = []
                for b in range(PIECES):
                    block = raw[k, t * PIECES + b]
                    parts += [block[0:1], block[1:2]]
                line = jnp.concatenate(parts, axis=1)
                at = 2 * t + k
                par_send[at : at + 1, :] = 1.0 / line if k == 0 else line
        pl.semaphore_wait(barrier, nctx - 1)
        for to in around:
            remote(
                par_send, par_recv.at[my_relay], send_sem.at[PAR], par_recv_sem.at[my_relay], to, p
            ).start()
        pltpu.make_async_copy(par_send, par_recv.at[my_relay], par_recv_sem.at[my_relay]).start()

    pos = iota((SUB, LANES), 0).astype(F32)
    eights = iota((tokens // SUB, LANES), 0).astype(F32) * SUB
    doc_first = doc_of(first)
    doc_last = doc_of(first + tokens - 1)
    at_start = jnp.where(doc_row == doc_first, 1.0, 0.0)
    at_end = jnp.where(doc_row == doc_last, 1.0, 0.0)

    def own_blocks(x):
        out = jnp.zeros((GROUP, LANES), F32)
        for g in range(TILE_GROUPS):
            both = x[2 * g * GROUP : (2 * g + 1) * GROUP] + x[(2 * g + 1) * GROUP : (2 * g + 2) * GROUP]
            out = jnp.where(block_of == g, fold(both), out)
        return out

    for a in range(relays):
        pltpu.make_async_copy(par_recv.at[a], par_recv.at[a], par_recv_sem.at[a]).wait()
        for t in range(relay_tiles):
            rates[a * relay_tiles + t] = par_recv[a, 2 * t : 2 * t + 1, :]
            weights[a * relay_tiles + t] = par_recv[a, 2 * t + 1 : 2 * t + 2, :]

    def states(q):
        rate_row = rates[q]
        tall = jnp.exp(-eights * rate_row)
        short = jnp.exp(-pos * rate_row)
        short_flip = jnp.exp((pos - (SUB - 1.0)) * rate_row)
        steps = tokens // SUB
        decay = jnp.concatenate([short * tall[i : i + 1] for i in range(steps)], axis=0)
        flip = jnp.concatenate(
            [short_flip * tall[steps - 1 - i : steps - i] for i in range(steps)], axis=0
        )
        end_state = own_blocks(dot(mix_t[q], wide(flip * at_end)))
        start_state = own_blocks(dot(dconv_t[q], wide(decay * at_start)))
        for r in range(PIECES):
            j = PIECES * q + r
            state_send[j, 0:ROWS, :] = end_state[r * ROWS : (r + 1) * ROWS, :]
            state_send[j, ROWS:, :] = start_state[r * ROWS : (r + 1) * ROWS, :]
        for r in range(PIECES):
            j = PIECES * q + r
            push(state_send.at[j], state_recv.at[c], STATE, j, p)

    sides = tiles // nx
    for dx in far_first(nx):
        for side in reversed(range(sides)):
            q_x = lax.rem(my_x + dx, nx) * sides
            states(q_x + lax.rem(lax.rem(tile_of, sides) + side, sides))

    for z in far_first(ntp):
        for a in range(relays):
            tp_to = lax.rem(p + z, ntp)
            push(corr_send.at[a * ntp + tp_to], corr_recv.at[c], CORR, p * relays + a, tp_to)

    lag = col.astype(F32)
    doc_before = doc_of(first - 1)
    doc_after = doc_of(first + tokens)
    upper = jnp.where(jnp.logical_and(doc_row == doc_col, col >= row), 1.0, 0.0)
    with_before = jnp.where(doc_col == doc_before, 1.0, 0.0)
    with_after = jnp.where(doc_col == doc_after, 1.0, 0.0)

    def quarters(x):
        return fold(x[:GROUP] + x[GROUP:])

    def inside(q, _):
        rate = jnp.broadcast_to(rates[q], square).T
        weight = jnp.broadcast_to(weights[q], square).T
        lead_wide[q] = wide(jnp.exp(-(lag + 1.0) * rate) * (weight * with_before))
        tail_wide[q] = wide(jnp.exp((lag - float(tokens)) * rate) * (weight * with_after))
        terms = jnp.exp(-lag * rate) * weight
        for g in range(TILE_GROUPS):
            taps = jnp.sum(terms[g * MODES : (g + 1) * MODES], axis=0, keepdims=True)
            spread = jnp.broadcast_to(taps, square)
            toeplitz = pltpu.roll(spread, 0, 1, stride=1, stride_axis=0) * upper
            high, low = halves(toeplitz)
            rows = slice(g * GROUP, (g + 1) * GROUP)
            both = slice(2 * g * GROUP, 2 * (g + 1) * GROUP)
            conv_t[q, rows, :] = quarters(
                dot(mix_t[q, both, :], jnp.concatenate([high, low], axis=1))
            )
            dmix_t[q, rows, :] = quarters(
                dot_nt(dconv_t[q, both, :], jnp.concatenate([high, low], axis=0))
            )
        return 0

    lax.fori_loop(0, tiles // 2, inside, 0)

    arrived(state_recv, STATE)
    my_rate = rates[tile_of]
    span = jnp.exp(-float(tokens) * my_rate)
    once = jnp.exp(-my_rate)
    piece = (2 * ROWS, LANES)
    cut_in = [jnp.full(piece, end // tokens, jnp.int32) for end in ends[:3]]
    cut_out = [jnp.full(piece, (end - 1) // tokens, jnp.int32) for end in ends[:3]]
    cut_at = [jnp.full(piece, end, jnp.int32) for end in ends[:3]]
    is_end = iota(piece, 0) < ROWS

    def kept(cuts, at, factor):
        hit = cuts[0] == at
        for cut in cuts[1:]:
            hit = jnp.logical_or(hit, cut == at)
        return jnp.where(hit, 0.0, factor)

    backs = [None] * nctx
    back = jnp.zeros(piece, F32)
    for i in range(nctx - 1, -1, -1):
        backs[i] = back
        back = kept(cut_out, i, span) * back + state_recv[i]
    ahead = jnp.zeros(piece, F32)
    carried = jnp.zeros(piece, F32)
    for i in range(nctx):
        here = state_recv[i]
        carry_send[i] = jnp.where(is_end, ahead, backs[i])
        begun = pltpu.roll(here, ROWS, 0)
        carried = carried + kept(cut_at, i * tokens, once) * (ahead * begun)
        ahead = kept(cut_in, i, span) * ahead + here
    for to in around:
        remote(
            carry_send.at[to], carry_recv.at[c], send_sem.at[CARRY], recv_sem.at[CARRY], to, p
        ).start()
    pltpu.make_async_copy(carry_send.at[c], carry_recv.at[c], recv_sem.at[CARRY]).start()
    carried = jnp.where(is_end, carried, 0.0)
    part_send[...] = jnp.sum(carried, axis=0, keepdims=True)
    for b in range(PIECES):
        block = tile_of * PIECES + b
        push(
            part_send,
            part_recv.at[piece_of],
            PART,
            p * relays + block // ntp,
            lax.rem(block, ntp),
        )

    lax.fori_loop(tiles // 2, tiles, inside, 0)

    loads[5].wait()
    loads[6].wait()
    arrived(corr_recv, CORR)

    def add_corr(i, total):
        return total + corr_recv[i]

    corr = lax.fori_loop(0, nctx, add_corr, jnp.zeros((OWN_GROUPS, LANES), F32))
    own_rate = 1.0 / own_par[0]
    own_rate = jnp.concatenate([own_rate[0:1], own_rate[1:2]] * PIECES, axis=1)
    powers = jnp.exp(-row.astype(F32) * own_rate)
    by_mode = fold(dot(wide(jnp.concatenate([corr] * PIECES, axis=0)), twice(wide(powers))))
    lane = iota((1, LANES), 1)
    grad_row = jnp.where(lax.rem(lane // MODES, OWN_GROUPS) == 0, by_mode[0:1], by_mode[1:2])
    arrived(part_recv, PART)
    for r in range(PIECES):
        grad_row = grad_row + part_recv[r]
    step = LANES // PIECES
    grad_row = jnp.where(lane // step == lax.rem(mine, PIECES), grad_row / seq_len, 0.0)
    whole = grad_row
    for b in range(1, PIECES):
        whole = whole + pltpu.roll(grad_row, b * step, 1)
    grad_res_ref[0:1, :] = whole[:, :MODES]
    grad_res_ref[1:2, :] = pltpu.roll(whole, LANES - MODES, 1)[:, :MODES]

    arrived(carry_recv, CARRY)

    def spread_out(q, rows):
        state = jnp.concatenate(
            [carry_recv[PIECES * q + r, rows, :] for r in range(PIECES)], axis=0
        )
        parts = []
        for half in halves(state):
            zero = jnp.zeros_like(half)
            parts.append(
                jnp.concatenate(
                    [jnp.where(block_of == g, half, zero) for g in range(TILE_GROUPS)], axis=0
                )
            )
        return jnp.concatenate(parts, axis=1)

    outs = (
        (mixed, mixed_hbm),
        (grad_query, grad_query_hbm),
        (grad_key, grad_key_hbm),
        (grad_value, grad_value_hbm),
    )
    stores = []
    for q in range(tiles):
        at = slice(q * LANES, (q + 1) * LANES)
        entered = fold(dot(spread_out(q, slice(0, ROWS)), twice(lead_wide[q])))
        conv = (conv_t[q] + entered).T
        mixed[:, at] = (query[:, at].astype(F32) * conv).astype(BF16)
        grad_query[:, at] = (grad[:, at].astype(F32) * conv).astype(BF16)
        left = fold(dot(spread_out(q, slice(ROWS, 2 * ROWS)), twice(tail_wide[q])))
        dmix = (dmix_t[q] + left).T
        grad_key[:, at] = (dmix * value[:, at].astype(F32)).astype(BF16)
        grad_value[:, at] = (dmix * key[:, at].astype(F32)).astype(BF16)
        for i, (src, dst) in enumerate(outs):
            copy = pltpu.make_async_copy(src.at[:, at], dst.at[:, at], store_sem.at[q, i])
            copy.start()
            stores.append(copy)

    sent(state_send.at[pl.ds(0, nctx - 1)], STATE)
    sent(carry_send.at[pl.ds(0, nctx - 1)], CARRY)

    @pl.when(is_relay)
    def _():
        for _ in range(nctx - 1):
            pltpu.make_async_copy(par_send, par_send, send_sem.at[PAR]).wait()
        sent(corr_send.at[pl.ds(0, nctx - 1)], CORR)

    @pl.when(jnp.logical_not(is_relay))
    def _():
        for k, src in enumerate((time_hbm, res_hbm)):
            pltpu.make_async_copy(src, src, raw_send_sem.at[k]).wait()
        sent(corr_send, CORR)

    to_self = jnp.logical_and(is_relay, mine // PIECES == tile_of)

    @pl.when(to_self)
    def _():
        sent(part_recv.at[pl.ds(0, PIECES - 1)], PART)

    @pl.when(jnp.logical_not(to_self))
    def _():
        sent(part_recv, PART)

    for copy in stores:
        copy.wait()


def copy_kernel(chunks, *refs):
    count = (len(refs) - 1) // 3
    sources, results = refs[:count], refs[count : 2 * count]
    stages, sem = refs[2 * count : 3 * count], refs[-1]
    loads, stores = [], []
    for i in range(count):
        rows = sources[i].shape[0]
        parts = chunks if rows % (16 * chunks) == 0 else 1
        for k in range(parts):
            at = pl.ds(k * (rows // parts), rows // parts)
            src, stage, dst = sources[i].at[at], stages[i].at[at], results[i].at[at]
            loads.append(pltpu.make_async_copy(src, stage, sem.at[0, i, k]))
            stores.append(pltpu.make_async_copy(stage, dst, sem.at[1, i, k]))
    for load in loads:
        load.start()
    for load, store in zip(loads, stores):
        load.wait()
        store.start()
    for store in stores:
        store.wait()


def per_device(nctx, ntp, query, key, value, grad, residues, decay_time, doc_lengths):
    tokens, channels = query.shape
    tiles = channels // LANES
    relays = nctx // ntp
    vmem = pl.BlockSpec(memory_space=pltpu.VMEM)
    hbm = pl.BlockSpec(memory_space=pl.ANY)
    flat = jax.ShapeDtypeStruct((tokens, channels), BF16)
    small = jax.ShapeDtypeStruct(residues.shape, F32)
    piece = pltpu.VMEM((nctx, 2 * ROWS, LANES), F32)
    lags = pltpu.VMEM((nctx, OWN_GROUPS, LANES), F32)
    line = pltpu.VMEM((tiles, 1, LANES), F32)
    outs = pl.pallas_call(
        functools.partial(exchange_kernel, nctx, ntp),
        out_shape=(flat, flat, flat, flat, small),
        in_specs=[hbm] * 7,
        out_specs=(hbm, hbm, hbm, hbm, vmem),
        scratch_shapes=[
            pltpu.SMEM(doc_lengths.shape, jnp.int32),
            *[pltpu.VMEM((tokens, channels), BF16)] * 8,
            pltpu.VMEM((2, ntp, OWN_GROUPS, MODES), F32),
            pltpu.VMEM((2 * tiles // relays, LANES), F32),
            pltpu.VMEM((relays, 2 * tiles // relays, LANES), F32),
            line,
            line,
            pltpu.VMEM((2, OWN_GROUPS, MODES), F32),
            *[pltpu.VMEM((tiles, 2 * LANES, tokens), BF16)] * 2,
            *[pltpu.VMEM((tiles, LANES, 2 * LANES), BF16)] * 2,
            *[pltpu.VMEM((tiles, LANES, LANES), F32)] * 2,
            piece,
            piece,
            piece,
            piece,
            lags,
            lags,
            pltpu.VMEM((1, LANES), F32),
            pltpu.VMEM((PIECES, 1, LANES), F32),
            pltpu.SemaphoreType.DMA((7,)),
            pltpu.SemaphoreType.DMA((tiles, 4)),
            pltpu.SemaphoreType.DMA((2,)),
            pltpu.SemaphoreType.DMA((2, ntp)),
            pltpu.SemaphoreType.DMA((relays,)),
            pltpu.SemaphoreType.DMA((5,)),
            pltpu.SemaphoreType.DMA((5,)),
        ],
        compiler_params=pltpu.CompilerParams(
            collective_id=0, has_side_effects=True, vmem_limit_bytes=64 * 1024 * 1024
        ),
    )(doc_lengths, query, key, value, grad, residues, decay_time)
    chunks = 1
    return tuple(
        pl.pallas_call(
            functools.partial(copy_kernel, chunks),
            out_shape=(flat, flat, flat, flat, small),
            in_specs=[hbm] * 5,
            out_specs=(hbm,) * 5,
            scratch_shapes=[
                *[pltpu.VMEM(flat.shape, BF16)] * 4,
                pltpu.VMEM(small.shape, F32),
                pltpu.SemaphoreType.DMA((2, 5, chunks)),
            ],
            compiler_params=pltpu.CompilerParams(vmem_limit_bytes=64 * 1024 * 1024),
        )(*outs)
    )


def solution(mesh):
    main = P("ctx", "tp")
    owned = P(("ctx", "tp"), None)
    return jax.shard_map(
        functools.partial(per_device, mesh.shape["ctx"], mesh.shape["tp"]),
        mesh=mesh,
        in_specs=(main, main, main, main, owned, owned, P()),
        out_specs=(main, main, main, main, owned),
        check_vma=False,
    )
```

time: 42.9 us -> 35.9 us (0.84)
  the two profiles are of different devices: /device:TPU:4 before, /device:TPU:29 now
where the time goes in v2:
time: 35.9 us; the launch traced here: 35.8 us
  Pallas kernels  35.1 us (98%)
  between operations  0.64 us (2%)
    pallas_call x1, Pallas kernels, per_device(): pl.pallas_call(functools.partial(exchange_kernel, nctx, ntp), out_shape=(...  33.1 us
    pallas_call x1, Pallas kernels, per_device(): pl.pallas_call(functools.partial(copy_kernel, chunks), out_shape=(flat, f...  2 us

profile of v2, /device:TPU:29, one launch (start us, length us, event | category | flops | bytes accessed | tf_op | source)
XLA Modules:
  0.0 35.8 jit_solution(15429203762701360525)
XLA Ops:
  0.6 33.1 %shard_map.110 = (bf16[128,1024]{1,0:T(8,128)(2,1)}, bf16[128,1024]{1,0:T(8,128)(2,1)}, bf16[128,1024]{1,0:T(8,128)(2,1)}, bf16[128,1024]{1,0:T(8,128)(2,1)}, f32[2,16]{1,0:T(2,128)}) custom-call(s32[4]{0:T(128)} %doc_hbm.1, bf16[128,1024]{1,0:T(8,128)(2,1)} %query_hbm.1, bf16[128,1024]{1,0:T(8,128)(2,1)} %key_hbm.1, bf16[128,1024]{1,0:T(8,128)(2,1)} %value_hbm.1, ...), custom_call_target="tpu_custom_call" | custom-call | tf_op jit(solution)/shard_map/pallas_call | solution.py:563
  33.8 2.0 %shard_map.111 = (bf16[128,1024]{1,0:T(8,128)(2,1)}, bf16[128,1024]{1,0:T(8,128)(2,1)}, bf16[128,1024]{1,0:T(8,128)(2,1)}, bf16[128,1024]{1,0:T(8,128)(2,1)}, f32[2,16]{1,0:T(2,128)}) custom-call(bf16[128,1024]{1,0:T(8,128)(2,1)} %get-tuple-element.10.refs_0_, bf16[128,1024]{1,0:T(8,128)(2,1)} %get-tuple-element.11.refs_1_, ...), custom_call_target="tpu_custom_call" | custom-call | tf_op jit(solution)/shard_map/pallas_call | solution.py:602

commit v3 on v2

--- a/solution.py
+++ b/solution.py
@@ -14,7 +14,8 @@
 TILE_GROUPS = LANES // GROUP
 OWN_GROUPS = 2
 PIECES = TILE_GROUPS // OWN_GROUPS
-ROWS = GROUP // PIECES
+SHARES = 4
+ROWS = GROUP // SHARES
 
 F32 = jnp.float32
 BF16 = jnp.bfloat16
@@ -83,20 +84,16 @@
     grad_hbm,
     res_hbm,
     time_hbm,
-    mixed_hbm,
-    grad_query_hbm,
-    grad_key_hbm,
-    grad_value_hbm,
+    mixed,
+    grad_query,
+    grad_key,
+    grad_value,
     grad_res_ref,
     doc_ref,
     query,
     key,
     value,
     grad,
-    mixed,
-    grad_query,
-    grad_key,
-    grad_value,
     raw,
     par_send,
     par_recv,
@@ -105,6 +102,7 @@
     own_par,
     mix_t,
     dconv_t,
+    mix_turned,
     lead_wide,
     tail_wide,
     conv_t,
@@ -118,7 +116,6 @@
     part_send,
     part_recv,
     load_sem,
-    store_sem,
     raw_send_sem,
     raw_recv_sem,
     par_recv_sem,
@@ -136,8 +133,8 @@
     plane = c // relays
     is_relay = plane == p
     mine = lax.rem(c, relays) * ntp + p
-    piece_of = lax.rem(c, PIECES)
-    tile_of = c // PIECES
+    share_of = lax.rem(c, SHARES)
+    tile_of = c // SHARES
     my_x = c // (2 * ny)
     my_y = lax.rem(c // 2, ny)
     my_core = lax.rem(c, 2)
@@ -210,7 +207,10 @@
                 src, raw.at[k, p], raw_send_sem.at[k], raw_recv_sem.at[k, p], c, plane
             ).start()
 
-    @pl.when(p > plane)
+    rank = jnp.minimum(p, ntp // 2)
+    behind = jnp.where(is_relay, -ntp, jnp.minimum(plane, ntp // 2) - rank)
+
+    @pl.when(jnp.logical_and(jnp.logical_not(is_relay), behind <= 0))
     def _():
         send_raw()
 
@@ -251,32 +251,52 @@
     def lanes_of(q):
         return pl.ds(pl.multiple_of(q * LANES, LANES), LANES)
 
-    def local(q, _):
+    def prepare(q, _):
         at = lanes_of(q)
         mixture = key[:, at].astype(F32) * value[:, at].astype(F32)
         dconv = grad[:, at].astype(F32) * query[:, at].astype(F32)
         mix_t[q] = stack_halves(mixture.T)
         dconv_t[q] = stack_halves(dconv.T)
-        d_high, d_low = halves(dconv)
-        right = jnp.concatenate(
-            [jnp.concatenate([d_high, d_high], axis=1), jnp.concatenate([d_low, d_low], axis=1)],
-            axis=0,
-        )
-        left = dot(turn, wide(mixture)).astype(BF16)
-        lane_block = lax.rem(iota((1, 2 * LANES), 1), LANES) // GROUP
-        for g in range(TILE_GROUPS):
-            masked = jnp.where(lane_block == g, left, jnp.zeros_like(left))
-            lags = pltpu.roll(
-                fold(dot_nt(masked, right)) * turned, 1, 1, stride=1, stride_axis=0
-            )
-            corr_send[PIECES * q + g // OWN_GROUPS, g % OWN_GROUPS : g % OWN_GROUPS + 1, :] = (
-                jnp.sum(lags, axis=0, keepdims=True)
-            )
+        mix_turned[q] = dot(turn, wide(mixture)).astype(BF16)
         return 0
 
-    lax.fori_loop(0, tiles, local, 0)
-
-    @pl.when(p < plane)
+    lax.fori_loop(0, tiles, prepare, 0)
+
+    def correlate(q, _):
+        nothing = jnp.zeros((GROUP, LANES), BF16)
+        half_groups = TILE_GROUPS // 2
+        half_lanes = LANES // 2
+        for h in range(2):
+            high = mix_turned[q, :, h * half_lanes : (h + 1) * half_lanes]
+            low = mix_turned[q, :, LANES + h * half_lanes : LANES + (h + 1) * half_lanes]
+            left = jnp.concatenate([high, low, high, low], axis=1)
+            for first_group in range(h * half_groups, (h + 1) * half_groups, 2):
+                columns = []
+                for g in (first_group, first_group + 1):
+                    rows = []
+                    for section in range(4):
+                        at = (2 * g + section // 2) * GROUP
+                        taken = dconv_t[q, at : at + GROUP, :]
+                        for other in range(h * half_groups, (h + 1) * half_groups):
+                            rows.append(taken if other == g else nothing)
+                    columns.append(jnp.concatenate(rows, axis=0))
+                pairs = dot(left, jnp.concatenate(columns, axis=1))
+                for k in range(OWN_GROUPS):
+                    lags = pltpu.roll(
+                        pairs[:, k * LANES : (k + 1) * LANES] * turned,
+                        1,
+                        1,
+                        stride=1,
+                        stride_axis=0,
+                    )
+                    block = PIECES * q + first_group // OWN_GROUPS
+                    corr_send[block, k : k + 1, :] = jnp.sum(lags, axis=0, keepdims=True)
+        return 0
+
+    early = jnp.where(behind > 2, tiles, 0)
+    lax.fori_loop(0, early, correlate, 0)
+
+    @pl.when(behind > 0)
     def _():
         send_raw()
 
@@ -303,6 +323,8 @@
             ).start()
         pltpu.make_async_copy(par_send, par_recv.at[my_relay], par_recv_sem.at[my_relay]).start()
 
+    lax.fori_loop(early, tiles, correlate, 0)
+
     pos = iota((SUB, LANES), 0).astype(F32)
     eights = iota((tokens // SUB, LANES), 0).astype(F32) * SUB
     doc_first = doc_of(first)
@@ -335,12 +357,12 @@
         )
         end_state = own_blocks(dot(mix_t[q], wide(flip * at_end)))
         start_state = own_blocks(dot(dconv_t[q], wide(decay * at_start)))
-        for r in range(PIECES):
-            j = PIECES * q + r
-            state_send[j, 0:ROWS, :] = end_state[r * ROWS : (r + 1) * ROWS, :]
-            state_send[j, ROWS:, :] = start_state[r * ROWS : (r + 1) * ROWS, :]
-        for r in range(PIECES):
-            j = PIECES * q + r
+        for h in range(SHARES):
+            j = SHARES * q + h
+            state_send[j, 0:ROWS, :] = end_state[h * ROWS : (h + 1) * ROWS, :]
+            state_send[j, ROWS:, :] = start_state[h * ROWS : (h + 1) * ROWS, :]
+        for h in range(SHARES):
+            j = SHARES * q + h
             push(state_send.at[j], state_recv.at[c], STATE, j, p)
 
     sides = tiles // nx
@@ -403,68 +425,43 @@
             hit = jnp.logical_or(hit, cut == at)
         return jnp.where(hit, 0.0, factor)
 
-    backs = [None] * nctx
     back = jnp.zeros(piece, F32)
-    for i in range(nctx - 1, -1, -1):
-        backs[i] = back
-        back = kept(cut_out, i, span) * back + state_recv[i]
     ahead = jnp.zeros(piece, F32)
+    backs, aheads = [None] * nctx, [None] * nctx
+    for i in range(nctx):
+        j = nctx - 1 - i
+        backs[j] = back
+        back = kept(cut_out, j, span) * back + state_recv[j]
+        aheads[i] = ahead
+        ahead = kept(cut_in, i, span) * ahead + state_recv[i]
     carried = jnp.zeros(piece, F32)
     for i in range(nctx):
-        here = state_recv[i]
-        carry_send[i] = jnp.where(is_end, ahead, backs[i])
-        begun = pltpu.roll(here, ROWS, 0)
-        carried = carried + kept(cut_at, i * tokens, once) * (ahead * begun)
-        ahead = kept(cut_in, i, span) * ahead + here
+        carry_send[i] = jnp.where(is_end, aheads[i], backs[i])
+        begun = pltpu.roll(state_recv[i], ROWS, 0)
+        carried = carried + kept(cut_at, i * tokens, once) * (aheads[i] * begun)
+    part_send[...] = jnp.sum(jnp.where(is_end, carried, 0.0), axis=0, keepdims=True)
+    for b in range(PIECES):
+        block = tile_of * PIECES + b
+        push(
+            part_send,
+            part_recv.at[share_of],
+            PART,
+            p * relays + block // ntp,
+            lax.rem(block, ntp),
+        )
     for to in around:
         remote(
             carry_send.at[to], carry_recv.at[c], send_sem.at[CARRY], recv_sem.at[CARRY], to, p
         ).start()
     pltpu.make_async_copy(carry_send.at[c], carry_recv.at[c], recv_sem.at[CARRY]).start()
-    carried = jnp.where(is_end, carried, 0.0)
-    part_send[...] = jnp.sum(carried, axis=0, keepdims=True)
-    for b in range(PIECES):
-        block = tile_of * PIECES + b
-        push(
-            part_send,
-            part_recv.at[piece_of],
-            PART,
-            p * relays + block // ntp,
-            lax.rem(block, ntp),
-        )
 
     lax.fori_loop(tiles // 2, tiles, inside, 0)
-
-    loads[5].wait()
-    loads[6].wait()
-    arrived(corr_recv, CORR)
-
-    def add_corr(i, total):
-        return total + corr_recv[i]
-
-    corr = lax.fori_loop(0, nctx, add_corr, jnp.zeros((OWN_GROUPS, LANES), F32))
-    own_rate = 1.0 / own_par[0]
-    own_rate = jnp.concatenate([own_rate[0:1], own_rate[1:2]] * PIECES, axis=1)
-    powers = jnp.exp(-row.astype(F32) * own_rate)
-    by_mode = fold(dot(wide(jnp.concatenate([corr] * PIECES, axis=0)), twice(wide(powers))))
-    lane = iota((1, LANES), 1)
-    grad_row = jnp.where(lax.rem(lane // MODES, OWN_GROUPS) == 0, by_mode[0:1], by_mode[1:2])
-    arrived(part_recv, PART)
-    for r in range(PIECES):
-        grad_row = grad_row + part_recv[r]
-    step = LANES // PIECES
-    grad_row = jnp.where(lane // step == lax.rem(mine, PIECES), grad_row / seq_len, 0.0)
-    whole = grad_row
-    for b in range(1, PIECES):
-        whole = whole + pltpu.roll(grad_row, b * step, 1)
-    grad_res_ref[0:1, :] = whole[:, :MODES]
-    grad_res_ref[1:2, :] = pltpu.roll(whole, LANES - MODES, 1)[:, :MODES]
 
     arrived(carry_recv, CARRY)
 
     def spread_out(q, rows):
         state = jnp.concatenate(
-            [carry_recv[PIECES * q + r, rows, :] for r in range(PIECES)], axis=0
+            [carry_recv[SHARES * q + h, rows, :] for h in range(SHARES)], axis=0
         )
         parts = []
         for half in halves(state):
@@ -476,13 +473,6 @@
             )
         return jnp.concatenate(parts, axis=1)
 
-    outs = (
-        (mixed, mixed_hbm),
-        (grad_query, grad_query_hbm),
-        (grad_key, grad_key_hbm),
-        (grad_value, grad_value_hbm),
-    )
-    stores = []
     for q in range(tiles):
         at = slice(q * LANES, (q + 1) * LANES)
         entered = fold(dot(spread_out(q, slice(0, ROWS)), twice(lead_wide[q])))
@@ -493,13 +483,43 @@
         dmix = (dmix_t[q] + left).T
         grad_key[:, at] = (dmix * value[:, at].astype(F32)).astype(BF16)
         grad_value[:, at] = (dmix * key[:, at].astype(F32)).astype(BF16)
-        for i, (src, dst) in enumerate(outs):
-            copy = pltpu.make_async_copy(src.at[:, at], dst.at[:, at], store_sem.at[q, i])
-            copy.start()
-            stores.append(copy)
+
+    loads[5].wait()
+    loads[6].wait()
+    arrived(corr_recv, CORR)
+
+    def add_corr(i, total):
+        return total + corr_recv[i]
+
+    corr = lax.fori_loop(0, nctx, add_corr, jnp.zeros((OWN_GROUPS, LANES), F32))
+    own_rate = 1.0 / own_par[0]
+    own_rate = jnp.concatenate([own_rate[0:1], own_rate[1:2]] * PIECES, axis=1)
+    powers = jnp.exp(-row.astype(F32) * own_rate)
+    by_mode = fold(dot(wide(jnp.concatenate([corr] * PIECES, axis=0)), twice(wide(powers))))
+    lane = iota((1, LANES), 1)
+    grad_row = jnp.where(lax.rem(lane // MODES, OWN_GROUPS) == 0, by_mode[0:1], by_mode[1:2])
+    arrived(part_recv, PART)
+    for h in range(SHARES):
+        grad_row = grad_row + part_recv[h]
+    step = LANES // PIECES
+    grad_row = jnp.where(lane // step == lax.rem(mine, PIECES), grad_row / seq_len, 0.0)
+    whole = grad_row
+    for b in range(1, PIECES):
+        whole = whole + pltpu.roll(grad_row, b * step, 1)
+    grad_res_ref[0:1, :] = whole[:, :MODES]
+    grad_res_ref[1:2, :] = pltpu.roll(whole, LANES - MODES, 1)[:, :MODES]
 
     sent(state_send.at[pl.ds(0, nctx - 1)], STATE)
     sent(carry_send.at[pl.ds(0, nctx - 1)], CARRY)
+    to_self = jnp.logical_and(is_relay, mine // PIECES == tile_of)
+
+    @pl.when(to_self)
+    def _():
+        sent(part_recv.at[pl.ds(0, PIECES - 1)], PART)
+
+    @pl.when(jnp.logical_not(to_self))
+    def _():
+        sent(part_recv, PART)
 
     @pl.when(is_relay)
     def _():
@@ -513,40 +533,16 @@
             pltpu.make_async_copy(src, src, raw_send_sem.at[k]).wait()
         sent(corr_send, CORR)
 
-    to_self = jnp.logical_and(is_relay, mine // PIECES == tile_of)
-
-    @pl.when(to_self)
-    def _():
-        sent(part_recv.at[pl.ds(0, PIECES - 1)], PART)
-
-    @pl.when(jnp.logical_not(to_self))
-    def _():
-        sent(part_recv, PART)
-
-    for copy in stores:
+
+def copy_kernel(*refs):
+    count = (len(refs) - 1) // 2
+    copies = [
+        pltpu.make_async_copy(refs[i], refs[count + i], refs[-1].at[i]) for i in range(count)
+    ]
+    for copy in copies:
+        copy.start()
+    for copy in copies:
         copy.wait()
-
-
-def copy_kernel(chunks, *refs):
-    count = (len(refs) - 1) // 3
-    sources, results = refs[:count], refs[count : 2 * count]
-    stages, sem = refs[2 * count : 3 * count], refs[-1]
-    loads, stores = [], []
-    for i in range(count):
-        rows = sources[i].shape[0]
-        parts = chunks if rows % (16 * chunks) == 0 else 1
-        for k in range(parts):
-            at = pl.ds(k * (rows // parts), rows // parts)
-            src, stage, dst = sources[i].at[at], stages[i].at[at], results[i].at[at]
-            loads.append(pltpu.make_async_copy(src, stage, sem.at[0, i, k]))
-            stores.append(pltpu.make_async_copy(stage, dst, sem.at[1, i, k]))
-    for load in loads:
-        load.start()
-    for load, store in zip(loads, stores):
-        load.wait()
-        store.start()
-    for store in stores:
-        store.wait()
 
 
 def per_device(nctx, ntp, query, key, value, grad, residues, decay_time, doc_lengths):
@@ -557,17 +553,18 @@
     hbm = pl.BlockSpec(memory_space=pl.ANY)
     flat = jax.ShapeDtypeStruct((tokens, channels), BF16)
     small = jax.ShapeDtypeStruct(residues.shape, F32)
-    piece = pltpu.VMEM((nctx, 2 * ROWS, LANES), F32)
+    by_device = pltpu.VMEM((nctx, 2 * ROWS, LANES), F32)
     lags = pltpu.VMEM((nctx, OWN_GROUPS, LANES), F32)
     line = pltpu.VMEM((tiles, 1, LANES), F32)
+    arguments = (doc_lengths, query, key, value, grad, residues, decay_time)
     outs = pl.pallas_call(
         functools.partial(exchange_kernel, nctx, ntp),
-        out_shape=(flat, flat, flat, flat, small),
+        out_shape=(*[pltpu.VMEM(flat.shape, BF16)] * 4, pltpu.VMEM(small.shape, F32)),
         in_specs=[hbm] * 7,
-        out_specs=(hbm, hbm, hbm, hbm, vmem),
+        out_specs=(vmem,) * 5,
         scratch_shapes=[
             pltpu.SMEM(doc_lengths.shape, jnp.int32),
-            *[pltpu.VMEM((tokens, channels), BF16)] * 8,
+            *[pltpu.VMEM((tokens, channels), BF16)] * 4,
             pltpu.VMEM((2, ntp, OWN_GROUPS, MODES), F32),
             pltpu.VMEM((2 * tiles // relays, LANES), F32),
             pltpu.VMEM((relays, 2 * tiles // relays, LANES), F32),
@@ -575,18 +572,14 @@
             line,
             pltpu.VMEM((2, OWN_GROUPS, MODES), F32),
             *[pltpu.VMEM((tiles, 2 * LANES, tokens), BF16)] * 2,
-            *[pltpu.VMEM((tiles, LANES, 2 * LANES), BF16)] * 2,
+            *[pltpu.VMEM((tiles, LANES, 2 * LANES), BF16)] * 3,
             *[pltpu.VMEM((tiles, LANES, LANES), F32)] * 2,
-            piece,
-            piece,
-            piece,
-            piece,
+            *[by_device] * 4,
             lags,
             lags,
             pltpu.VMEM((1, LANES), F32),
-            pltpu.VMEM((PIECES, 1, LANES), F32),
+            pltpu.VMEM((SHARES, 1, LANES), F32),
             pltpu.SemaphoreType.DMA((7,)),
-            pltpu.SemaphoreType.DMA((tiles, 4)),
             pltpu.SemaphoreType.DMA((2,)),
             pltpu.SemaphoreType.DMA((2, ntp)),
             pltpu.SemaphoreType.DMA((relays,)),
@@ -594,23 +587,18 @@
             pltpu.SemaphoreType.DMA((5,)),
         ],
         compiler_params=pltpu.CompilerParams(
-            collective_id=0, has_side_effects=True, vmem_limit_bytes=64 * 1024 * 1024
+            collective_id=0, has_side_effects=True, vmem_limit_bytes=32 * 1024 * 1024
         ),
-    )(doc_lengths, query, key, value, grad, residues, decay_time)
-    chunks = 1
+    )(*[pltpu.with_memory_space_constraint(x, pltpu.HBM) for x in arguments])
     return tuple(
         pl.pallas_call(
-            functools.partial(copy_kernel, chunks),
+            copy_kernel,
             out_shape=(flat, flat, flat, flat, small),
             in_specs=[hbm] * 5,
             out_specs=(hbm,) * 5,
-            scratch_shapes=[
-                *[pltpu.VMEM(flat.shape, BF16)] * 4,
-                pltpu.VMEM(small.shape, F32),
-                pltpu.SemaphoreType.DMA((2, 5, chunks)),
-            ],
-            compiler_params=pltpu.CompilerParams(vmem_limit_bytes=64 * 1024 * 1024),
-        )(*outs)
+            scratch_shapes=[pltpu.SemaphoreType.DMA((5,))],
+            compiler_params=pltpu.CompilerParams(vmem_limit_bytes=1024 * 1024),
+        )(*[pltpu.with_memory_space_constraint(x, pltpu.VMEM) for x in outs])
     )
 
 

time: 35.9 us -> 31.2 us (0.87)
  the two profiles are of different devices: /device:TPU:29 before, /device:TPU:4 now
where the time goes in v3:
time: 31.2 us; the launch traced here: 31.1 us
  Pallas kernels  30.5 us (98%)
  between operations  0.64 us (2%)
    pallas_call x1, Pallas kernels, per_device(): pl.pallas_call(functools.partial(exchange_kernel, nctx, ntp), out_shape=(...  29.5 us
    pallas_call x1, Pallas kernels, per_device(): pl.pallas_call(copy_kernel, out_shape=(flat, flat, flat, flat, small), in...  1.01 us

profile of v3, /device:TPU:4, one launch (start us, length us, event | category | flops | bytes accessed | tf_op | source)
XLA Modules:
  0.0 31.1 jit_solution(7495588724059382590)
XLA Ops:
  0.6 29.5 %shard_map.110 = (bf16[128,1024]{1,0:T(8,128)(2,1)S(1)}, bf16[128,1024]{1,0:T(8,128)(2,1)S(1)}, bf16[128,1024]{1,0:T(8,128)(2,1)S(1)}, bf16[128,1024]{1,0:T(8,128)(2,1)S(1)}, f32[2,16]{1,0:T(2,128)S(1)}) custom-call(s32[4]{0:T(128)} %doc_hbm.1, bf16[128,1024]{1,0:T(8,128)(2,1)} %query_hbm.1, bf16[128,1024]{1,0:T(8,128)(2,1)} %key_hbm.1, ...), custom_call_target="tpu_custom_call" | custom-call | tf_op jit(solution)/shard_map/pallas_call | solution.py:560
  30.1 1.0 %shard_map.111 = (bf16[128,1024]{1,0:T(8,128)(2,1)}, bf16[128,1024]{1,0:T(8,128)(2,1)}, bf16[128,1024]{1,0:T(8,128)(2,1)}, bf16[128,1024]{1,0:T(8,128)(2,1)}, f32[2,16]{1,0:T(2,128)}) custom-call(bf16[128,1024]{1,0:T(8,128)(2,1)S(1)} %get-tuple-element.10.refs_0_, bf16[128,1024]{1,0:T(8,128)(2,1)S(1)} %get-tuple-element.11.refs_1_, ...), custom_call_target="tpu_custom_call" | custom-call | tf_op jit(solution)/shard_map/pallas_call | solution.py:594

commit v4 on v3

--- a/solution.py
+++ b/solution.py
@@ -72,6 +72,21 @@
 
 def far_first(n):
     return sorted(range(n), key=lambda d: -min(d, n - d))
+
+
+def scan_places(tiles, nx, ny):
+    if (tiles, nx, ny) == (8, 4, 4):
+        return (
+            ((0, 0), (0, 3)),
+            ((2, 0), (1, 3)),
+            ((1, 0), (3, 0)),
+            ((3, 3), (2, 3)),
+            ((0, 1), (0, 2)),
+            ((2, 1), (1, 2)),
+            ((1, 1), (3, 1)),
+            ((3, 2), (2, 2)),
+        )
+    return tuple(tuple(divmod(2 * q + k, ny) for k in range(2)) for q in range(tiles))
 
 
 def exchange_kernel(
@@ -102,6 +117,8 @@
     own_par,
     mix_t,
     dconv_t,
+    mix_k,
+    dconv_k,
     mix_turned,
     lead_wide,
     tail_wide,
@@ -133,8 +150,6 @@
     plane = c // relays
     is_relay = plane == p
     mine = lax.rem(c, relays) * ntp + p
-    share_of = lax.rem(c, SHARES)
-    tile_of = c // SHARES
     my_x = c // (2 * ny)
     my_y = lax.rem(c // 2, ny)
     my_core = lax.rem(c, 2)
@@ -166,6 +181,52 @@
     def sent(ref, kind):
         pltpu.make_async_copy(ref, ref, send_sem.at[kind]).wait()
 
+    sources = (query_hbm, key_hbm, value_hbm, grad_hbm, doc_hbm, time_hbm, res_hbm)
+    targets = (query, key, value, grad, doc_ref, own_par.at[0], own_par.at[1])
+    loads = [
+        pltpu.make_async_copy(src, dst, load_sem.at[i])
+        for i, (src, dst) in enumerate(zip(sources, targets))
+    ]
+    for i in (5, 6, 4, 1, 2, 0, 3):
+        loads[i].start()
+    barrier = pltpu.get_barrier_semaphore()
+
+    def greet(ctx_to, tp_to):
+        pl.semaphore_signal(barrier, inc=1, device_id=(ctx_to, tp_to), device_id_type=MESH)
+
+    @pl.when(is_relay)
+    def _():
+        for d in far_first(ntp):
+            if d:
+                greet(c, lax.rem(p + d, ntp))
+
+    for a in range(relays):
+        relay = p * relays + a
+
+        @pl.when(relay != c)
+        def _():
+            greet(relay, p)
+
+    loads[5].wait()
+    loads[6].wait()
+
+    base_x = (p * relays // 2) // ny
+    base_y = lax.rem(p * relays // 2, ny)
+    places = scan_places(tiles, nx, ny)
+
+    def scanner(q, h):
+        dx, dy = places[q][h // 2]
+        x, y = lax.rem(base_x + dx, nx), lax.rem(base_y + dy, ny)
+        return (x * ny + y) * 2 + h % 2
+
+    tile_of = jnp.int32(0)
+    share_of = my_core
+    for q in range(tiles):
+        for k in range(2):
+            hit = scanner(q, 2 * k) == c - my_core
+            tile_of = jnp.where(hit, q, tile_of)
+            share_of = jnp.where(hit, 2 * k + my_core, share_of)
+
     xs = [lax.rem(my_x + d, nx) * (2 * ny) for d in range(nx)]
     ys = [lax.rem(my_y + d, ny) * 2 for d in range(ny)]
     cores = [my_core, 1 - my_core]
@@ -173,39 +234,9 @@
     offsets.sort(key=lambda o: -(min(o[0], nx - o[0]) + min(o[1], ny - o[1]) + 0.1 * o[2]))
     around = [xs[dx] + ys[dy] + cores[dk] for dx, dy, dk in offsets if dx or dy or dk]
 
-    barrier = pltpu.get_barrier_semaphore()
-
-    def greet(ctx_to, tp_to):
-        pl.semaphore_signal(barrier, inc=1, device_id=(ctx_to, tp_to), device_id_type=MESH)
-
-    @pl.when(is_relay)
-    def _():
-        for d in far_first(ntp):
-            if d:
-                greet(c, lax.rem(p + d, ntp))
-
-    for a in range(relays):
-        relay = p * relays + a
-
-        @pl.when(relay != c)
-        def _():
-            greet(relay, p)
-
-    sources = (query_hbm, key_hbm, value_hbm, grad_hbm, doc_hbm, time_hbm, res_hbm)
-    targets = (query, key, value, grad, doc_ref, own_par.at[0], own_par.at[1])
-    loads = [
-        pltpu.make_async_copy(src, dst, load_sem.at[i])
-        for i, (src, dst) in enumerate(zip(sources, targets))
-    ]
-    for i in (4, 1, 2, 0, 3, 5, 6):
-        loads[i].start()
-
     def send_raw():
         pl.semaphore_wait(barrier, 1)
-        for k, src in enumerate((time_hbm, res_hbm)):
-            remote(
-                src, raw.at[k, p], raw_send_sem.at[k], raw_recv_sem.at[k, p], c, plane
-            ).start()
+        remote(own_par, raw.at[p], raw_send_sem, raw_recv_sem.at[p], c, plane).start()
 
     rank = jnp.minimum(p, ntp // 2)
     behind = jnp.where(is_relay, -ntp, jnp.minimum(plane, ntp // 2) - rank)
@@ -216,8 +247,7 @@
 
     @pl.when(is_relay)
     def _():
-        for k, src in enumerate((time_hbm, res_hbm)):
-            pltpu.make_async_copy(src, raw.at[k, p], raw_recv_sem.at[k, p]).start()
+        raw[p] = own_par[...]
 
     first = c * tokens
     loads[4].wait()
@@ -256,7 +286,9 @@
         mixture = key[:, at].astype(F32) * value[:, at].astype(F32)
         dconv = grad[:, at].astype(F32) * query[:, at].astype(F32)
         mix_t[q] = stack_halves(mixture.T)
+        mix_k[q] = wide(mixture.T)
         dconv_t[q] = stack_halves(dconv.T)
+        dconv_k[q] = wide(dconv.T)
         mix_turned[q] = dot(turn, wide(mixture)).astype(BF16)
         return 0
 
@@ -304,14 +336,14 @@
 
     @pl.when(is_relay)
     def _():
-        for k, src in enumerate((time_hbm, res_hbm)):
-            for z in range(ntp):
-                pltpu.make_async_copy(src, raw.at[k, z], raw_recv_sem.at[k, z]).wait()
+        for d in range(1, ntp):
+            z = lax.rem(p + d, ntp)
+            pltpu.make_async_copy(own_par, raw.at[z], raw_recv_sem.at[z]).wait()
         for t in range(relay_tiles):
             for k in range(2):
                 parts = []
                 for b in range(PIECES):
-                    block = raw[k, t * PIECES + b]
+                    block = raw[t * PIECES + b, k]
                     parts += [block[0:1], block[1:2]]
                 line = jnp.concatenate(parts, axis=1)
                 at = 2 * t + k
@@ -335,8 +367,7 @@
     def own_blocks(x):
         out = jnp.zeros((GROUP, LANES), F32)
         for g in range(TILE_GROUPS):
-            both = x[2 * g * GROUP : (2 * g + 1) * GROUP] + x[(2 * g + 1) * GROUP : (2 * g + 2) * GROUP]
-            out = jnp.where(block_of == g, fold(both), out)
+            out = jnp.where(block_of == g, fold(x[g * GROUP : (g + 1) * GROUP]), out)
         return out
 
     for a in range(relays):
@@ -355,21 +386,20 @@
         flip = jnp.concatenate(
             [short_flip * tall[steps - 1 - i : steps - i] for i in range(steps)], axis=0
         )
-        end_state = own_blocks(dot(mix_t[q], wide(flip * at_end)))
-        start_state = own_blocks(dot(dconv_t[q], wide(decay * at_start)))
+        end_state = own_blocks(dot(mix_k[q], twice(wide(flip * at_end))))
+        start_state = own_blocks(dot(dconv_k[q], twice(wide(decay * at_start))))
         for h in range(SHARES):
-            j = SHARES * q + h
-            state_send[j, 0:ROWS, :] = end_state[h * ROWS : (h + 1) * ROWS, :]
-            state_send[j, ROWS:, :] = start_state[h * ROWS : (h + 1) * ROWS, :]
-        for h in range(SHARES):
-            j = SHARES * q + h
-            push(state_send.at[j], state_recv.at[c], STATE, j, p)
-
-    sides = tiles // nx
-    for dx in far_first(nx):
-        for side in reversed(range(sides)):
-            q_x = lax.rem(my_x + dx, nx) * sides
-            states(q_x + lax.rem(lax.rem(tile_of, sides) + side, sides))
+            to = scanner(q, h)
+            state_send[to, 0:ROWS, :] = end_state[h * ROWS : (h + 1) * ROWS, :]
+            state_send[to, ROWS:, :] = start_state[h * ROWS : (h + 1) * ROWS, :]
+
+    for q in range(tiles):
+        states(q)
+    for to in around:
+        remote(
+            state_send.at[to], state_recv.at[c], send_sem.at[STATE], recv_sem.at[STATE], to, p
+        ).start()
+    pltpu.make_async_copy(state_send.at[c], state_recv.at[c], recv_sem.at[STATE]).start()
 
     for z in far_first(ntp):
         for a in range(relays):
@@ -461,7 +491,7 @@
 
     def spread_out(q, rows):
         state = jnp.concatenate(
-            [carry_recv[SHARES * q + h, rows, :] for h in range(SHARES)], axis=0
+            [carry_recv[scanner(q, h), rows, :] for h in range(SHARES)], axis=0
         )
         parts = []
         for half in halves(state):
@@ -484,8 +514,6 @@
         grad_key[:, at] = (dmix * value[:, at].astype(F32)).astype(BF16)
         grad_value[:, at] = (dmix * key[:, at].astype(F32)).astype(BF16)
 
-    loads[5].wait()
-    loads[6].wait()
     arrived(corr_recv, CORR)
 
     def add_corr(i, total):
@@ -529,8 +557,7 @@
 
     @pl.when(jnp.logical_not(is_relay))
     def _():
-        for k, src in enumerate((time_hbm, res_hbm)):
-            pltpu.make_async_copy(src, src, raw_send_sem.at[k]).wait()
+        pltpu.make_async_copy(own_par, own_par, raw_send_sem).wait()
         sent(corr_send, CORR)
 
 
@@ -565,14 +592,14 @@
         scratch_shapes=[
             pltpu.SMEM(doc_lengths.shape, jnp.int32),
             *[pltpu.VMEM((tokens, channels), BF16)] * 4,
-            pltpu.VMEM((2, ntp, OWN_GROUPS, MODES), F32),
+            pltpu.VMEM((ntp, 2, OWN_GROUPS, MODES), F32),
             pltpu.VMEM((2 * tiles // relays, LANES), F32),
             pltpu.VMEM((relays, 2 * tiles // relays, LANES), F32),
             line,
             line,
             pltpu.VMEM((2, OWN_GROUPS, MODES), F32),
             *[pltpu.VMEM((tiles, 2 * LANES, tokens), BF16)] * 2,
-            *[pltpu.VMEM((tiles, LANES, 2 * LANES), BF16)] * 3,
+            *[pltpu.VMEM((tiles, LANES, 2 * LANES), BF16)] * 5,
             *[pltpu.VMEM((tiles, LANES, LANES), F32)] * 2,
             *[by_device] * 4,
             lags,
@@ -580,8 +607,8 @@
             pltpu.VMEM((1, LANES), F32),
             pltpu.VMEM((SHARES, 1, LANES), F32),
             pltpu.SemaphoreType.DMA((7,)),
-            pltpu.SemaphoreType.DMA((2,)),
-            pltpu.SemaphoreType.DMA((2, ntp)),
+            pltpu.SemaphoreType.DMA,
+            pltpu.SemaphoreType.DMA((ntp,)),
             pltpu.SemaphoreType.DMA((relays,)),
             pltpu.SemaphoreType.DMA((5,)),
             pltpu.SemaphoreType.DMA((5,)),

time: 31.2 us -> 29.9 us (0.958)
  Pallas kernels: 30.5 us -> 29 us
    pallas_call x1, Pallas kernels: 29.5 us -> 28 us  [per_device(): pl.pallas_call(functools.partial(exchange_kernel, nctx, ntp), out_shape=(...]
where the time goes in v4:
time: 29.9 us; the launch traced here: 29.6 us
  Pallas kernels  29 us (97%)
  between operations  0.64 us (2%)
    pallas_call x1, Pallas kernels, per_device(): pl.pallas_call(functools.partial(exchange_kernel, nctx, ntp), out_shape=(...  28 us
    pallas_call x1, Pallas kernels, per_device(): pl.pallas_call(copy_kernel, out_shape=(flat, flat, flat, flat, small), in...  1.01 us

profile of v4, /device:TPU:4, one launch (start us, length us, event | category | flops | bytes accessed | tf_op | source)
XLA Modules:
  0.0 29.6 jit_solution(8739674496884061212)
XLA Ops:
  0.6 28.0 %shard_map.110 = (bf16[128,1024]{1,0:T(8,128)(2,1)S(1)}, bf16[128,1024]{1,0:T(8,128)(2,1)S(1)}, bf16[128,1024]{1,0:T(8,128)(2,1)S(1)}, bf16[128,1024]{1,0:T(8,128)(2,1)S(1)}, f32[2,16]{1,0:T(2,128)S(1)}) custom-call(s32[4]{0:T(128)} %doc_hbm.1, bf16[128,1024]{1,0:T(8,128)(2,1)} %query_hbm.1, bf16[128,1024]{1,0:T(8,128)(2,1)} %key_hbm.1, ...), custom_call_target="tpu_custom_call" | custom-call | tf_op jit(solution)/shard_map/pallas_call | solution.py:587
  28.6 1.0 %shard_map.111 = (bf16[128,1024]{1,0:T(8,128)(2,1)}, bf16[128,1024]{1,0:T(8,128)(2,1)}, bf16[128,1024]{1,0:T(8,128)(2,1)}, bf16[128,1024]{1,0:T(8,128)(2,1)}, f32[2,16]{1,0:T(2,128)}) custom-call(bf16[128,1024]{1,0:T(8,128)(2,1)S(1)} %get-tuple-element.10.refs_0_, bf16[128,1024]{1,0:T(8,128)(2,1)S(1)} %get-tuple-element.11.refs_1_, ...), custom_call_target="tpu_custom_call" | custom-call | tf_op jit(solution)/shard_map/pallas_call | solution.py:621

commit v5 on v4

--- a/solution.py
+++ b/solution.py
@@ -130,6 +130,7 @@
     carry_recv,
     corr_send,
     corr_recv,
+    powers_wide,
     part_send,
     part_recv,
     load_sem,
@@ -194,11 +195,29 @@
     def greet(ctx_to, tp_to):
         pl.semaphore_signal(barrier, inc=1, device_id=(ctx_to, tp_to), device_id_type=MESH)
 
+    half = ntp // 2
+    hub = jnp.where(plane < 3 * ntp // 4, ntp // 4, 0)
+    by_hub = plane >= half
+    is_hub = jnp.logical_and(by_hub, p == hub)
+    low = jnp.logical_and(by_hub, p < half)
+
     @pl.when(is_relay)
     def _():
         for d in far_first(ntp):
             if d:
-                greet(c, lax.rem(p + d, ntp))
+                z = lax.rem(p + d, ntp)
+
+                @pl.when(jnp.logical_not(jnp.logical_and(by_hub, jnp.logical_and(z < half, z != hub))))
+                def _():
+                    greet(c, z)
+
+    @pl.when(is_hub)
+    def _():
+        for z in range(half):
+
+            @pl.when(z != hub)
+            def _():
+                greet(c, z)
 
     for a in range(relays):
         relay = p * relays + a
@@ -207,8 +226,6 @@
         def _():
             greet(relay, p)
 
-    loads[5].wait()
-    loads[6].wait()
 
     base_x = (p * relays // 2) // ny
     base_y = lax.rem(p * relays // 2, ny)
@@ -236,16 +253,26 @@
 
     def send_raw():
         pl.semaphore_wait(barrier, 1)
-        remote(own_par, raw.at[p], raw_send_sem, raw_recv_sem.at[p], c, plane).start()
-
-    rank = jnp.minimum(p, ntp // 2)
-    behind = jnp.where(is_relay, -ntp, jnp.minimum(plane, ntp // 2) - rank)
-
-    @pl.when(jnp.logical_and(jnp.logical_not(is_relay), behind <= 0))
+        remote(own_par, raw.at[p], raw_send_sem, raw_recv_sem.at[p], c, raw_to).start()
+
+    collects = jnp.logical_or(is_relay, is_hub)
+    raw_to = jnp.where(low, hub, plane)
+    behind = jnp.where(collects, -ntp, jnp.minimum(raw_to, half) - jnp.minimum(p, half))
+
+    @pl.when(jnp.logical_and(jnp.logical_not(collects), behind < 0))
+    def _():
+        pl.semaphore_wait(barrier, 1)
+        for k, src in enumerate((time_hbm, res_hbm)):
+            remote(src, raw.at[p, k], raw_send_sem, raw_recv_sem.at[p], c, raw_to).start()
+
+    loads[5].wait()
+    loads[6].wait()
+
+    @pl.when(behind == 0)
     def _():
         send_raw()
 
-    @pl.when(is_relay)
+    @pl.when(collects)
     def _():
         raw[p] = own_par[...]
 
@@ -332,13 +359,39 @@
     def _():
         send_raw()
 
+    lower = raw.at[pl.ds(0, half)]
+
+    @pl.when(is_hub)
+    def _():
+        for z in range(half):
+
+            @pl.when(z != hub)
+            def _():
+                pltpu.make_async_copy(own_par, raw.at[z], raw_recv_sem.at[z]).wait()
+
+        pl.semaphore_wait(barrier, 1)
+        remote(lower, lower, raw_send_sem, raw_recv_sem.at[hub], c, plane).start()
+
     my_relay = lax.rem(c, relays)
 
     @pl.when(is_relay)
     def _():
-        for d in range(1, ntp):
-            z = lax.rem(p + d, ntp)
-            pltpu.make_async_copy(own_par, raw.at[z], raw_recv_sem.at[z]).wait()
+        for z in range(half):
+
+            @pl.when(jnp.logical_not(jnp.logical_or(by_hub, z == p)))
+            def _():
+                pltpu.make_async_copy(own_par, raw.at[z], raw_recv_sem.at[z]).wait()
+
+        @pl.when(by_hub)
+        def _():
+            pltpu.make_async_copy(lower, lower, raw_recv_sem.at[hub]).wait()
+
+        for z in range(half, ntp):
+
+            @pl.when(z != p)
+            def _():
+                pltpu.make_async_copy(own_par, raw.at[z], raw_recv_sem.at[z]).wait()
+
         for t in range(relay_tiles):
             for k in range(2):
                 parts = []
@@ -487,6 +540,11 @@
 
     lax.fori_loop(tiles // 2, tiles, inside, 0)
 
+    own_rate = 1.0 / own_par[0]
+    own_rate = jnp.concatenate([own_rate[0:1], own_rate[1:2]] * PIECES, axis=1)
+    powers = jnp.exp(-row.astype(F32) * own_rate)
+    powers_wide[...] = wide(powers)
+
     arrived(carry_recv, CARRY)
 
     def spread_out(q, rows):
@@ -516,14 +574,11 @@
 
     arrived(corr_recv, CORR)
 
-    def add_corr(i, total):
-        return total + corr_recv[i]
-
-    corr = lax.fori_loop(0, nctx, add_corr, jnp.zeros((OWN_GROUPS, LANES), F32))
-    own_rate = 1.0 / own_par[0]
-    own_rate = jnp.concatenate([own_rate[0:1], own_rate[1:2]] * PIECES, axis=1)
-    powers = jnp.exp(-row.astype(F32) * own_rate)
-    by_mode = fold(dot(wide(jnp.concatenate([corr] * PIECES, axis=0)), twice(wide(powers))))
+    sums = [corr_recv[i] for i in range(nctx)]
+    while len(sums) > 1:
+        sums = [sums[i] + sums[i + 1] for i in range(0, len(sums), 2)]
+    corr = sums[0]
+    by_mode = fold(dot(wide(jnp.concatenate([corr] * PIECES, axis=0)), twice(powers_wide[...])))
     lane = iota((1, LANES), 1)
     grad_row = jnp.where(lax.rem(lane // MODES, OWN_GROUPS) == 0, by_mode[0:1], by_mode[1:2])
     arrived(part_recv, PART)
@@ -557,8 +612,15 @@
 
     @pl.when(jnp.logical_not(is_relay))
     def _():
+        sent(corr_send, CORR)
+
+    @pl.when(jnp.logical_not(collects))
+    def _():
         pltpu.make_async_copy(own_par, own_par, raw_send_sem).wait()
-        sent(corr_send, CORR)
+
+    @pl.when(is_hub)
+    def _():
+        pltpu.make_async_copy(lower, lower, raw_send_sem).wait()
 
 
 def copy_kernel(*refs):
@@ -604,6 +666,7 @@
             *[by_device] * 4,
             lags,
             lags,
+            pltpu.VMEM((tokens, 2 * LANES), BF16),
             pltpu.VMEM((1, LANES), F32),
             pltpu.VMEM((SHARES, 1, LANES), F32),
             pltpu.SemaphoreType.DMA((7,)),

time: 29.9 us -> 28.3 us (0.946)
  Pallas kernels: 29 us -> 27.3 us
    pallas_call x1, Pallas kernels: 28 us -> 26.3 us  [per_device(): pl.pallas_call(functools.partial(exchange_kernel, nctx, ntp), out_shape=(...]
where the time goes in v5:
time: 28.3 us; the launch traced here: 27.9 us
  Pallas kernels  27.3 us (96%)
  between operations  0.64 us (2%)
    pallas_call x1, Pallas kernels, per_device(): pl.pallas_call(functools.partial(exchange_kernel, nctx, ntp), out_shape=(...  26.3 us
    pallas_call x1, Pallas kernels, per_device(): pl.pallas_call(copy_kernel, out_shape=(flat, flat, flat, flat, small), in...  1.01 us

profile of v5, /device:TPU:4, one launch (start us, length us, event | category | flops | bytes accessed | tf_op | source)
XLA Modules:
  0.0 27.9 jit_solution(14515511616710308446)
XLA Ops:
  0.6 26.3 %shard_map.110 = (bf16[128,1024]{1,0:T(8,128)(2,1)S(1)}, bf16[128,1024]{1,0:T(8,128)(2,1)S(1)}, bf16[128,1024]{1,0:T(8,128)(2,1)S(1)}, bf16[128,1024]{1,0:T(8,128)(2,1)S(1)}, f32[2,16]{1,0:T(2,128)S(1)}) custom-call(s32[4]{0:T(128)} %doc_hbm.1, bf16[128,1024]{1,0:T(8,128)(2,1)} %query_hbm.1, bf16[128,1024]{1,0:T(8,128)(2,1)} %key_hbm.1, ...), custom_call_target="tpu_custom_call" | custom-call | tf_op jit(solution)/shard_map/pallas_call | solution.py:649
  26.9 1.0 %shard_map.111 = (bf16[128,1024]{1,0:T(8,128)(2,1)}, bf16[128,1024]{1,0:T(8,128)(2,1)}, bf16[128,1024]{1,0:T(8,128)(2,1)}, bf16[128,1024]{1,0:T(8,128)(2,1)}, f32[2,16]{1,0:T(2,128)}) custom-call(bf16[128,1024]{1,0:T(8,128)(2,1)S(1)} %get-tuple-element.10.refs_0_, bf16[128,1024]{1,0:T(8,128)(2,1)S(1)} %get-tuple-element.11.refs_1_, ...), custom_call_target="tpu_custom_call" | custom-call | tf_op jit(solution)/shard_map/pallas_call | solution.py:684

commit v6 on v5

--- a/solution.py
+++ b/solution.py
@@ -182,6 +182,53 @@
     def sent(ref, kind):
         pltpu.make_async_copy(ref, ref, send_sem.at[kind]).wait()
 
+    barrier = pltpu.get_barrier_semaphore()
+
+    def greet(ctx_to, tp_to):
+        pl.semaphore_signal(barrier, inc=1, device_id=(ctx_to, tp_to), device_id_type=MESH)
+
+    half = ntp // 2
+    hub = jnp.where(plane == 4, 2, 0)
+    by_hub = plane >= half
+    is_hub = jnp.logical_and(by_hub, p == hub)
+    low = jnp.logical_and(by_hub, p < half)
+
+    @pl.when(is_relay)
+    def _():
+        for d in far_first(ntp):
+            if d:
+                z = lax.rem(p + d, ntp)
+
+                @pl.when(jnp.logical_not(jnp.logical_and(by_hub, jnp.logical_and(z < half, z != hub))))
+                def _():
+                    greet(c, z)
+
+    @pl.when(is_hub)
+    def _():
+        for z in range(half):
+
+            @pl.when(z != hub)
+            def _():
+                greet(c, z)
+
+    for a in range(relays):
+        relay = p * relays + a
+
+        @pl.when(relay != c)
+        def _():
+            greet(relay, p)
+
+
+    collects = jnp.logical_or(is_relay, is_hub)
+    raw_to = jnp.where(low, hub, plane)
+    behind = jnp.where(collects, -ntp, jnp.minimum(raw_to, half) - jnp.minimum(p, half))
+
+    @pl.when(jnp.logical_and(jnp.logical_not(collects), behind < 0))
+    def _():
+        pl.semaphore_wait(barrier, 1)
+        for k, src in enumerate((time_hbm, res_hbm)):
+            remote(src, raw.at[p, k], raw_send_sem, raw_recv_sem.at[p], c, raw_to).start()
+
     sources = (query_hbm, key_hbm, value_hbm, grad_hbm, doc_hbm, time_hbm, res_hbm)
     targets = (query, key, value, grad, doc_ref, own_par.at[0], own_par.at[1])
     loads = [
@@ -190,43 +237,6 @@
     ]
     for i in (5, 6, 4, 1, 2, 0, 3):
         loads[i].start()
-    barrier = pltpu.get_barrier_semaphore()
-
-    def greet(ctx_to, tp_to):
-        pl.semaphore_signal(barrier, inc=1, device_id=(ctx_to, tp_to), device_id_type=MESH)
-
-    half = ntp // 2
-    hub = jnp.where(plane < 3 * ntp // 4, ntp // 4, 0)
-    by_hub = plane >= half
-    is_hub = jnp.logical_and(by_hub, p == hub)
-    low = jnp.logical_and(by_hub, p < half)
-
-    @pl.when(is_relay)
-    def _():
-        for d in far_first(ntp):
-            if d:
-                z = lax.rem(p + d, ntp)
-
-                @pl.when(jnp.logical_not(jnp.logical_and(by_hub, jnp.logical_and(z < half, z != hub))))
-                def _():
-                    greet(c, z)
-
-    @pl.when(is_hub)
-    def _():
-        for z in range(half):
-
-            @pl.when(z != hub)
-            def _():
-                greet(c, z)
-
-    for a in range(relays):
-        relay = p * relays + a
-
-        @pl.when(relay != c)
-        def _():
-            greet(relay, p)
-
-
     base_x = (p * relays // 2) // ny
     base_y = lax.rem(p * relays // 2, ny)
     places = scan_places(tiles, nx, ny)
@@ -254,16 +264,6 @@
     def send_raw():
         pl.semaphore_wait(barrier, 1)
         remote(own_par, raw.at[p], raw_send_sem, raw_recv_sem.at[p], c, raw_to).start()
-
-    collects = jnp.logical_or(is_relay, is_hub)
-    raw_to = jnp.where(low, hub, plane)
-    behind = jnp.where(collects, -ntp, jnp.minimum(raw_to, half) - jnp.minimum(p, half))
-
-    @pl.when(jnp.logical_and(jnp.logical_not(collects), behind < 0))
-    def _():
-        pl.semaphore_wait(barrier, 1)
-        for k, src in enumerate((time_hbm, res_hbm)):
-            remote(src, raw.at[p, k], raw_send_sem, raw_recv_sem.at[p], c, raw_to).start()
 
     loads[5].wait()
     loads[6].wait()
@@ -532,10 +532,14 @@
             p * relays + block // ntp,
             lax.rem(block, ntp),
         )
-    for to in around:
-        remote(
-            carry_send.at[to], carry_recv.at[c], send_sem.at[CARRY], recv_sem.at[CARRY], to, p
-        ).start()
+    for to in range(nctx):
+
+        @pl.when(to != c)
+        def _():
+            remote(
+                carry_send.at[to], carry_recv.at[c], send_sem.at[CARRY], recv_sem.at[CARRY], to, p
+            ).start()
+
     pltpu.make_async_copy(carry_send.at[c], carry_recv.at[c], recv_sem.at[CARRY]).start()
 
     lax.fori_loop(tiles // 2, tiles, inside, 0)

time: 28.3 us -> 28.2 us (level)
  no operation moved by 1% of the time
where the time goes in v6:
time: 28.2 us; the launch traced here: 27.9 us
  Pallas kernels  27.3 us (97%)
  between operations  0.64 us (2%)
    pallas_call x1, Pallas kernels, per_device(): pl.pallas_call(functools.partial(exchange_kernel, nctx, ntp), out_shape=(...  26.3 us
    pallas_call x1, Pallas kernels, per_device(): pl.pallas_call(copy_kernel, out_shape=(flat, flat, flat, flat, small), in...  1.01 us

profile of v6, /device:TPU:4, one launch (start us, length us, event | category | flops | bytes accessed | tf_op | source)
XLA Modules:
  0.0 27.9 jit_solution(15254514308163656183)
XLA Ops:
  0.6 26.3 %shard_map.110 = (bf16[128,1024]{1,0:T(8,128)(2,1)S(1)}, bf16[128,1024]{1,0:T(8,128)(2,1)S(1)}, bf16[128,1024]{1,0:T(8,128)(2,1)S(1)}, bf16[128,1024]{1,0:T(8,128)(2,1)S(1)}, f32[2,16]{1,0:T(2,128)S(1)}) custom-call(s32[4]{0:T(128)} %doc_hbm.1, bf16[128,1024]{1,0:T(8,128)(2,1)} %query_hbm.1, bf16[128,1024]{1,0:T(8,128)(2,1)} %key_hbm.1, ...), custom_call_target="tpu_custom_call" | custom-call | tf_op jit(solution)/shard_map/pallas_call | solution.py:653
  26.9 1.0 %shard_map.111 = (bf16[128,1024]{1,0:T(8,128)(2,1)}, bf16[128,1024]{1,0:T(8,128)(2,1)}, bf16[128,1024]{1,0:T(8,128)(2,1)}, bf16[128,1024]{1,0:T(8,128)(2,1)}, f32[2,16]{1,0:T(2,128)}) custom-call(bf16[128,1024]{1,0:T(8,128)(2,1)S(1)} %get-tuple-element.10.refs_0_, bf16[128,1024]{1,0:T(8,128)(2,1)S(1)} %get-tuple-element.11.refs_1_, ...), custom_call_target="tpu_custom_call" | custom-call | tf_op jit(solution)/shard_map/pallas_call | solution.py:688

commit v7 on v6

--- a/solution.py
+++ b/solution.py
@@ -532,14 +532,11 @@
             p * relays + block // ntp,
             lax.rem(block, ntp),
         )
-    for to in range(nctx):
-
-        @pl.when(to != c)
-        def _():
-            remote(
-                carry_send.at[to], carry_recv.at[c], send_sem.at[CARRY], recv_sem.at[CARRY], to, p
-            ).start()
-
+    for i in range(nctx - 1):
+        to = jnp.where(c <= i, i + 1, i)
+        remote(
+            carry_send.at[to], carry_recv.at[c], send_sem.at[CARRY], recv_sem.at[CARRY], to, p
+        ).start()
     pltpu.make_async_copy(carry_send.at[c], carry_recv.at[c], recv_sem.at[CARRY]).start()
 
     lax.fori_loop(tiles // 2, tiles, inside, 0)

time: 28.2 us -> 28.2 us (level)
  no operation moved by 1% of the time
where the time goes in v7:
time: 28.2 us; the launch traced here: 27.9 us
  Pallas kernels  27.3 us (97%)
  between operations  0.64 us (2%)
    pallas_call x1, Pallas kernels, per_device(): pl.pallas_call(functools.partial(exchange_kernel, nctx, ntp), out_shape=(...  26.3 us
    pallas_call x1, Pallas kernels, per_device(): pl.pallas_call(copy_kernel, out_shape=(flat, flat, flat, flat, small), in...  1.01 us

profile of v7, /device:TPU:4, one launch (start us, length us, event | category | flops | bytes accessed | tf_op | source)
XLA Modules:
  0.0 27.9 jit_solution(16102623277961594292)
XLA Ops:
  0.6 26.3 %shard_map.110 = (bf16[128,1024]{1,0:T(8,128)(2,1)S(1)}, bf16[128,1024]{1,0:T(8,128)(2,1)S(1)}, bf16[128,1024]{1,0:T(8,128)(2,1)S(1)}, bf16[128,1024]{1,0:T(8,128)(2,1)S(1)}, f32[2,16]{1,0:T(2,128)S(1)}) custom-call(s32[4]{0:T(128)} %doc_hbm.1, bf16[128,1024]{1,0:T(8,128)(2,1)} %query_hbm.1, bf16[128,1024]{1,0:T(8,128)(2,1)} %key_hbm.1, ...), custom_call_target="tpu_custom_call" | custom-call | tf_op jit(solution)/shard_map/pallas_call | solution.py:650
  26.9 1.0 %shard_map.111 = (bf16[128,1024]{1,0:T(8,128)(2,1)}, bf16[128,1024]{1,0:T(8,128)(2,1)}, bf16[128,1024]{1,0:T(8,128)(2,1)}, bf16[128,1024]{1,0:T(8,128)(2,1)}, f32[2,16]{1,0:T(2,128)}) custom-call(bf16[128,1024]{1,0:T(8,128)(2,1)S(1)} %get-tuple-element.10.refs_0_, bf16[128,1024]{1,0:T(8,128)(2,1)S(1)} %get-tuple-element.11.refs_1_, ...), custom_call_target="tpu_custom_call" | custom-call | tf_op jit(solution)/shard_map/pallas_call | solution.py:685

commit v8 on v7

--- a/solution.py
+++ b/solution.py
@@ -519,7 +519,6 @@
         ahead = kept(cut_in, i, span) * ahead + state_recv[i]
     carried = jnp.zeros(piece, F32)
     for i in range(nctx):
-        carry_send[i] = jnp.where(is_end, aheads[i], backs[i])
         begun = pltpu.roll(state_recv[i], ROWS, 0)
         carried = carried + kept(cut_at, i * tokens, once) * (aheads[i] * begun)
     part_send[...] = jnp.sum(jnp.where(is_end, carried, 0.0), axis=0, keepdims=True)
@@ -532,6 +531,8 @@
             p * relays + block // ntp,
             lax.rem(block, ntp),
         )
+    for i in range(nctx):
+        carry_send[i] = jnp.where(is_end, aheads[i], backs[i])
     for i in range(nctx - 1):
         to = jnp.where(c <= i, i + 1, i)
         remote(

time: 28.2 us -> 28.2 us (level)
  no operation moved by 1% of the time
where the time goes in v8:
time: 28.2 us; the launch traced here: 27.9 us
  Pallas kernels  27.3 us (97%)
  between operations  0.64 us (2%)
    pallas_call x1, Pallas kernels, per_device(): pl.pallas_call(functools.partial(exchange_kernel, nctx, ntp), out_shape=(...  26.3 us
    pallas_call x1, Pallas kernels, per_device(): pl.pallas_call(copy_kernel, out_shape=(flat, flat, flat, flat, small), in...  1.01 us

profile of v8, /device:TPU:4, one launch (start us, length us, event | category | flops | bytes accessed | tf_op | source)
XLA Modules:
  0.0 27.9 jit_solution(5488305384410253537)
XLA Ops:
  0.6 26.3 %shard_map.110 = (bf16[128,1024]{1,0:T(8,128)(2,1)S(1)}, bf16[128,1024]{1,0:T(8,128)(2,1)S(1)}, bf16[128,1024]{1,0:T(8,128)(2,1)S(1)}, bf16[128,1024]{1,0:T(8,128)(2,1)S(1)}, f32[2,16]{1,0:T(2,128)S(1)}) custom-call(s32[4]{0:T(128)} %doc_hbm.1, bf16[128,1024]{1,0:T(8,128)(2,1)} %query_hbm.1, bf16[128,1024]{1,0:T(8,128)(2,1)} %key_hbm.1, ...), custom_call_target="tpu_custom_call" | custom-call | tf_op jit(solution)/shard_map/pallas_call | solution.py:651
  26.9 1.0 %shard_map.111 = (bf16[128,1024]{1,0:T(8,128)(2,1)}, bf16[128,1024]{1,0:T(8,128)(2,1)}, bf16[128,1024]{1,0:T(8,128)(2,1)}, bf16[128,1024]{1,0:T(8,128)(2,1)}, f32[2,16]{1,0:T(2,128)}) custom-call(bf16[128,1024]{1,0:T(8,128)(2,1)S(1)} %get-tuple-element.10.refs_0_, bf16[128,1024]{1,0:T(8,128)(2,1)S(1)} %get-tuple-element.11.refs_1_, ...), custom_call_target="tpu_custom_call" | custom-call | tf_op jit(solution)/shard_map/pallas_call | solution.py:686
